TPU v7x, 512 devices: a whole 4x4x16 slice. The times are simulated.
512 devices in a mesh: band: 32 (over y_hi, z), gx: 8 (over x, core), gy: 2 (over y_lo).
Axes of the slice: x: 4, y: 4 (y_hi: 2, y_lo: 2; y = y_hi * 2 + y_lo), z: 16, core: 2. Of those that a mesh axis runs over, the one named last changes fastest.
Arguments:
- orbitals: float32 [256, 48, 16, 128], P('band', 'gx', 'gy'), may hold values from -120 to 120
- potential: float32 [48, 16, 128], P('gx', 'gy'), may hold values from -6 to 2
Outputs:
- rotated: float32 [256, 48, 16, 128], P('band', 'gx', 'gy')
- gram: float32 [256, 256], P('band')
All inputs are finite; a program needn't handle non-finite values.
Results may differ from a plain program's by a relative error of at most 0.0095.
Values may be sent and summed in bfloat16 or wider, within the bound.
A program may use at most 64 MiB of HBM per device.

v0:
```python
import jax
import jax.numpy as jnp
from jax import lax
from jax.sharding import PartitionSpec as P

stencil_coeffs = (
    -5369.0 / 1800.0,
    12.0 / 7.0,
    -15.0 / 56.0,
    10.0 / 189.0,
    -1.0 / 112.0,
    2.0 / 1925.0,
    -1.0 / 16632.0,
)
spacing = 0.5
low_edge = 5.0
high_edge = 46.0
bottom_edge = -6.5


def extended(shard, sides, width):
    for axis, dim in sides:
        devices, length = (lax.axis_size(axis), shard.shape[dim])
        up = [(i, (i + 1) % devices) for i in range(devices)]
        down = [(j, i) for i, j in up]
        last = lax.slice_in_dim(shard, length - width, length, axis=dim)
        leading = lax.slice_in_dim(shard, 0, width, axis=dim)
        before = lax.ppermute(last, axis, up)
        after = lax.ppermute(leading, axis, down)
        shard = jnp.concatenate([before, shard, after], axis=dim)
    return shard


def filter_scalars():
    half = (high_edge - low_edge) / 2.0
    center = (high_edge + low_edge) / 2.0
    sigma = half / (bottom_edge - center)
    sigma_two = 1.0 / (2.0 / sigma - sigma)
    return (half, center, sigma, sigma_two)


def apply_ham(field, potential):
    padded = extended(field, (("gx", 1), ("gy", 2)), 6)
    size_x = field.shape[1]
    size_y = field.shape[2]
    laplace = 3.0 * stencil_coeffs[0] * field
    for shift_by in range(1, 7):
        coeff = stencil_coeffs[shift_by]
        laplace = laplace + coeff * (
            padded[:, 6 + shift_by : 6 + shift_by + size_x, 6 : 6 + size_y]
            + padded[:, 6 - shift_by : 6 - shift_by + size_x, 6 : 6 + size_y]
        )
        laplace = laplace + coeff * (
            padded[:, 6 : 6 + size_x, 6 + shift_by : 6 + shift_by + size_y]
            + padded[:, 6 : 6 + size_x, 6 - shift_by : 6 - shift_by + size_y]
        )
        laplace = laplace + coeff * (jnp.roll(field, shift_by, 3) + jnp.roll(field, -shift_by, 3))
    return -0.5 / spacing**2 * laplace + potential[None] * field


def finish_coeffs(gram):
    count = gram.shape[0]
    lower = jnp.linalg.cholesky(gram)
    inv_lower = jax.scipy.linalg.solve_triangular(
        lower, jnp.eye(count, dtype=jnp.float32), lower=True
    )
    return inv_lower.T.astype(jnp.bfloat16)


def body(orbitals, potential):
    half, center, sigma, sigma_two = filter_scalars()
    first = sigma / half * (apply_ham(orbitals, potential) - center * orbitals)
    second = (
        2.0 * sigma_two / half * (apply_ham(first, potential) - center * first)
        - sigma * sigma_two * orbitals
    )
    local_count = orbitals.shape[0]
    mine = second.astype(jnp.bfloat16).reshape(local_count, -1)
    total_cells = mine.shape[1] * lax.axis_size("gx") * lax.axis_size("gy")
    shares = lax.all_to_all(mine, "band", split_axis=1, concat_axis=0, tiled=True)
    partial_gram = lax.dot_general(
        shares, shares, (((1,), (1,)), ((), ())), preferred_element_type=jnp.float32
    )
    summed = lax.psum(partial_gram, ("band", "gx", "gy"))
    gram = summed / total_cells
    coeffs = finish_coeffs(gram)
    rotated_share = lax.dot_general(
        coeffs, shares, (((0,), (0,)), ((), ())), preferred_element_type=jnp.float32
    )
    rotated = lax.all_to_all(
        rotated_share.astype(jnp.bfloat16), "band", split_axis=0, concat_axis=1, tiled=True
    ).astype(rotated_share.dtype)
    gram_rows = lax.dynamic_slice_in_dim(gram, lax.axis_index("band") * local_count, local_count, 0)
    return (rotated.reshape(orbitals.shape), gram_rows)


def solution(mesh):
    return jax.shard_map(
        body,
        mesh=mesh,
        in_specs=(P("band", "gx", "gy", None), P("gx", "gy", None)),
        out_specs=(P("band", "gx", "gy", None), P("band", None)),
        check_vma=False,
    )
```

profile of v0, /device:TPU:24, one launch (start us, length us, event | category | flops | bytes accessed | tf_op | source)
XLA Modules:
  0.0 651.4 jit_solution(1150979625307803435)
XLA Ops:
  7.2 1.0 copy.97
  8.2 2.9 collective-permute-start
  12.5 2.0 collective-permute-done.1
  14.8 2.7 collective-permute-start.2
  17.4 3.2 collective-permute-start.3
  20.8 8.9 %collective-permute-done.2 = f32[8,18,6,128]{3,0,2,1:T(8,128)S(1)} collective-permute-done((f32[8,18,6,128]{3,0,2,1:T(8,128)S(1)}, f32[8,18,6,128]{3,0,2,1:T(8,128)S(1)}, u32[]{:S(2)}, u32[]{:S(2)}) %collective-permute-start.2) | collective-permute-done | bytes 442400 | tf_op jit(solution)/shard_map/ppermute | solution.py:29
  29.7 8.8 %collective-permute-done.3 = f32[8,18,6,128]{3,0,2,1:T(8,128)S(1)} collective-permute-done((f32[8,18,6,128]{3,0,2,1:T(8,128)S(1)}, f32[8,18,6,128]{3,0,2,1:T(8,128)S(1)}, u32[]{:S(2)}, u32[]{:S(2)}) %collective-permute-start.3) | collective-permute-done | bytes 442400 | tf_op jit(solution)/shard_map/ppermute | solution.py:28
  38.5 1.0 broadcast_multiply_fusion.1
  39.5 1.7 collective-permute-start.4
  42.4 2.0 collective-permute-done.4
  44.4 3.1 collective-permute-done.5
  47.6 2.7 collective-permute-start.6
  50.3 3.2 collective-permute-start.7
  53.7 8.9 %collective-permute-done.6 = f32[8,18,6,128]{3,0,2,1:T(8,128)S(1)} collective-permute-done((f32[8,18,6,128]{3,0,2,1:T(8,128)S(1)}, f32[8,18,6,128]{3,0,2,1:T(8,128)S(1)}, u32[]{:S(2)}, u32[]{:S(2)}) %collective-permute-start.6) | collective-permute-done | bytes 442400 | tf_op jit(solution)/shard_map/ppermute | solution.py:29
  62.6 5.0 collective-permute-done.7
  67.7 1.0 subtract_convert_fusion
  69.0 32.4 %all_to_all.32 = bf16[8,32,192]{2,0,1:T(8,128)(2,1)S(1)} all-to-all(bf16[8,32,192]{2,0,1:T(8,128)(2,1)S(1)} %copy.131), channel_id=1, replica_groups=mesh['band'=32,'gx'=8,'gy'=2] {'band'}, dimensions={1} | all-to-all | bytes 196608 | tf_op jit(solution)/shard_map/all_to_all | solution.py:80
  101.4 0.9 fusion.110
  102.4 451.1 %all-reduce.3.cloned.1.call-done = f32[256,256]{0,1:T(8,128)} async-done(((f32[256,256]{0,1:T(8,128)}), f32[256,256]{0,1:T(8,128)}) %all-reduce.3.cloned.1.call-update) | async-done | bytes 262160 | tf_op jit(solution)/shard_map/psum | solution.py:84
  553.5 1.0 broadcast_multiply_fusion
  554.6 0.8 copy-done.1
  555.5 11.7 %cholesky.50 = f32[128,128]{1,0:T(8,128)S(1)} custom-call(f32[128,128]{1,0:T(8,128)S(1)} %cholesky.118), custom_call_target="Cholesky" | custom-call | tf_op jit(solution)/shard_map/jit(cholesky)/cholesky | solution.py:63
  567.2 9.8 %custom-call.15 = f32[1,128,128]{1,2,0:T(8,128)S(1)} custom-call(f32[1,128,128]{2,1,0:T(8,128)S(1)} %get-tuple-element.98), custom_call_target="InvertDiagBlocksLowerTriangular" | custom-call | tf_op jit(solution)/shard_map/jit(cholesky)/cholesky | solution.py:63
  577.5 11.7 %cholesky.105 = f32[128,128]{1,0:T(8,128)S(1)} custom-call(f32[128,128]{1,0:T(8,128)S(1)} %convolution_subtract_fusion.1), custom_call_target="Cholesky" | custom-call | tf_op jit(solution)/shard_map/jit(cholesky)/cholesky | solution.py:63
  591.3 3.9 while.1
  591.9 1.4 bitcast_dynamic-update-slice_fusion.2
  593.9 1.4 bitcast_dynamic-update-slice_fusion.2
  595.3 19.9 %custom-call.16 = f32[2,128,128]{1,2,0:T(8,128)S(1)} custom-call(f32[2,128,128]{2,1,0:T(8,128)S(1)} %get-tuple-element.9), custom_call_target="InvertDiagBlocksLowerTriangular" | custom-call | tf_op jit(solution)/shard_map/jit(_solve_triangular)/triangular_solve | solution.py:64
  616.3 0.8 copy.134
  617.0 9.8 %all-to-all-start.1 = ((bf16[32,8,192]{2,1,0:T(8,128)(2,1)}), bf16[32,8,192]{2,1,0:T(8,128)(2,1)S(1)}, u32[]{:S(2)}, u32[]{:S(2)}) async-start(bf16[32,8,192]{2,1,0:T(8,128)(2,1)} %bitcast.7), calls=%async_computation.1 | async-start | bytes 262144 | tf_op jit(solution)/shard_map/all_to_all | solution.py:90
  627.6 16.0 %all-to-all-done.1 = bf16[32,8,192]{2,1,0:T(8,128)(2,1)S(1)} async-done(((bf16[32,8,192]{2,1,0:T(8,128)(2,1)}), bf16[32,8,192]{2,1,0:T(8,128)(2,1)S(1)}, u32[]{:S(2)}, u32[]{:S(2)}) %all-to-all-start.1) | async-done | bytes 98336 | tf_op jit(solution)/shard_map/all_to_all | solution.py:90
  643.7 0.8 reshape.55
  (71 shorter events, 8.1 us)
Async XLA Ops:
  7.2 546.3 %all-reduce.3.cloned.1.call-start = ((), (), s32[]{:S(2)}) async-start(), calls=%async_computation.2 | async-start | bytes 524288 | tf_op jit(solution)/shard_map/psum | solution.py:84
  8.2 6.3 collective-permute-start.1
  8.2 6.4 collective-permute-start
  12.5 2.0 copy-start
  14.7 5.9 copy-start.2
  14.8 14.9 %collective-permute-start.2 = (f32[8,18,6,128]{3,0,2,1:T(8,128)S(1)}, f32[8,18,6,128]{3,0,2,1:T(8,128)S(1)}, u32[]{:S(2)}, u32[]{:S(2)}) collective-permute-start(f32[8,18,6,128]{3,0,2,1:T(8,128)S(1)} %get-tuple-element.38), channel_id=1, source_target_pairs={{1,0},{0,1},{3,2},{2,3},{5,4},{4,5},{7,6},{6,7},{9,8},{8,9},{11,10... | collective-permute-start | bytes 1327112 | tf_op jit(solution)/shard_map/ppermute | solution.py:29
  17.4 21.0 %collective-permute-start.3 = (f32[8,18,6,128]{3,0,2,1:T(8,128)S(1)}, f32[8,18,6,128]{3,0,2,1:T(8,128)S(1)}, u32[]{:S(2)}, u32[]{:S(2)}) collective-permute-start(f32[8,18,6,128]{3,0,2,1:T(8,128)S(1)} %get-tuple-element.39), channel_id=1, source_target_pairs={{0,1},{1,0},{2,3},{3,2},{4,5},{5,4},{6,7},{7,6},{8,9},{9,8},{10,11... | collective-permute-start | bytes 1327112 | tf_op jit(solution)/shard_map/ppermute | solution.py:28
  39.5 4.9 collective-permute-start.4
  41.2 6.3 collective-permute-start.5
  47.6 15.0 %collective-permute-start.6 = (f32[8,18,6,128]{3,0,2,1:T(8,128)S(1)}, f32[8,18,6,128]{3,0,2,1:T(8,128)S(1)}, u32[]{:S(2)}, u32[]{:S(2)}) collective-permute-start(f32[8,18,6,128]{3,0,2,1:T(8,128)S(1)} %get-tuple-element.36), channel_id=1, source_target_pairs={{1,0},{0,1},{3,2},{2,3},{5,4},{4,5},{7,6},{6,7},{9,8},{8,9},{11,10... | collective-permute-start | bytes 1327112 | tf_op jit(solution)/shard_map/ppermute | solution.py:29
  50.3 17.3 %collective-permute-start.7 = (f32[8,18,6,128]{3,0,2,1:T(8,128)S(1)}, f32[8,18,6,128]{3,0,2,1:T(8,128)S(1)}, u32[]{:S(2)}, u32[]{:S(2)}) collective-permute-start(f32[8,18,6,128]{3,0,2,1:T(8,128)S(1)} %get-tuple-element.37), channel_id=1, source_target_pairs={{0,1},{1,0},{2,3},{3,2},{4,5},{5,4},{6,7},{7,6},{8,9},{9,8},{10,11... | collective-permute-start | bytes 1327112 | tf_op jit(solution)/shard_map/ppermute | solution.py:28
  554.5 1.0 copy-start.1
  617.0 26.6 %all-to-all-start.1 = ((bf16[32,8,192]{2,1,0:T(8,128)(2,1)}), bf16[32,8,192]{2,1,0:T(8,128)(2,1)S(1)}, u32[]{:S(2)}, u32[]{:S(2)}) async-start(bf16[32,8,192]{2,1,0:T(8,128)(2,1)} %bitcast.7), calls=%async_computation.1 | async-start | bytes 262144 | tf_op jit(solution)/shard_map/all_to_all | solution.py:90
Sparse Core Ops, SparseCore 0:
  102.5 450.9 all-reduce.2
where the time goes:
time: 656 us; the launch traced here: 651 us
  waiting for transfers between devices  506 us (77%)
  other arithmetic  57.2 us (9%)
  blocking collectives  32.4 us (5%)
  starting transfers between devices  26.2 us (4%)
  between operations  15.8 us (2%)
  local copies, waits for them, and re-layouts  11.6 us (2%)
    psum x1, waiting for transfers between devices, body(): summed = lax.psum(partial_gram, ('band', 'gx', 'gy'))  451 us
    another operation x6, other arithmetic, finish_coeffs(): lower = jnp.linalg.cholesky(gram)  34 us
    all_to_all x1, blocking collectives, body(): lax.all_to_all(mine, 'band', split_axis=1, concat_axis=0, tiled=True)  32.4 us
    another operation x3, other arithmetic, finish_coeffs(): jax.scipy.linalg.solve_triangular(lower, jnp.eye(count, dtype=jnp.float32...  19.9 us
    ppermute x4, waiting for transfers between devices, extended(): after = lax.ppermute(leading, axis, down)  19.8 us
    ppermute x4, waiting for transfers between devices, extended(): before = lax.ppermute(last, axis, up)  18.9 us
    all_to_all x1, waiting for transfers between devices, body(): lax.all_to_all(rotated_share.astype(jnp.bfloat16), 'band', split_axis=0,...  16 us
  transfers between devices with their start and end apart: 10, of which 9 were waited for; matrix products, arithmetic and copies ran while one was open for 1% of the time, Pallas kernels for 0%

commit v1 on v0

--- a/solution.py
+++ b/solution.py
@@ -1,6 +1,10 @@
+import functools
+
 import jax
 import jax.numpy as jnp
 from jax import lax
+from jax.experimental import pallas as pl
+from jax.experimental.pallas import tpu as pltpu
 from jax.sharding import PartitionSpec as P
 
 stencil_coeffs = (
@@ -67,6 +71,297 @@
     return inv_lower.T.astype(jnp.bfloat16)
 
 
+MESH = pl.DeviceIdType.MESH
+BANDS = 32
+OWNERS = 24
+PLACES = 16
+GRID_Y = 2
+FULL = 256
+
+
+def owner_band(share):
+    return (share // 3) * 4 + share % 3
+
+
+def band_share(band):
+    return (band // 4) * 3 + band % 4
+
+
+def place_of(index):
+    return {"gx": index // GRID_Y, "gy": index % GRID_Y}
+
+
+def await_arrivals(buffer, sem):
+    pltpu.make_async_copy(buffer, buffer, sem).wait()
+
+
+def gram_kernel(
+    cells,
+    mine_ref,
+    gram_ref,
+    share_ref,
+    shares,
+    partial,
+    pieces,
+    piece,
+    rows,
+    total,
+    strips,
+    strip,
+    blocks,
+    send_sem,
+    recv_sem,
+    local_sem,
+):
+    band = lax.axis_index("band")
+    place = lax.axis_index("gx") * GRID_Y + lax.axis_index("gy")
+    owns = band % 4 != 3
+
+    barrier = pltpu.get_barrier_semaphore()
+
+    def greet_band(step, carry):
+        pl.semaphore_signal(
+            barrier, 1, device_id={"band": (band + step) % BANDS}, device_id_type=MESH
+        )
+        return carry
+
+    def greet_place(step, carry):
+        pl.semaphore_signal(
+            barrier, 1, device_id=place_of((place + step) % PLACES), device_id_type=MESH
+        )
+        return carry
+
+    lax.fori_loop(1, BANDS, greet_band, 0)
+    lax.fori_loop(1, PLACES, greet_place, 0)
+    pl.semaphore_wait(barrier, BANDS - 1 + PLACES - 1)
+
+    def remote(source, target, phase, device):
+        return pltpu.make_async_remote_copy(
+            src_ref=source,
+            dst_ref=target,
+            send_sem=send_sem.at[phase],
+            recv_sem=recv_sem.at[phase],
+            device_id=device,
+            device_id_type=MESH,
+        )
+
+    def cell_share(step, carry):
+        other = (band + step) % BANDS
+
+        @pl.when(other % 4 != 3)
+        def _():
+            at = pl.multiple_of(band_share(other) * 16, 16)
+            to = pl.multiple_of(band * 16, 16)
+            remote(
+                mine_ref.at[pl.ds(at, 16)], shares.at[pl.ds(to, 16)], 0, {"band": other}
+            ).start()
+
+        return carry
+
+    lax.fori_loop(1, BANDS, cell_share, 0)
+
+    @pl.when(owns)
+    def _():
+        at = pl.multiple_of(band_share(band) * 16, 16)
+        to = pl.multiple_of(band * 16, 16)
+        own = pltpu.make_async_copy(
+            mine_ref.at[pl.ds(at, 16)], shares.at[pl.ds(to, 16)], local_sem
+        )
+        own.start()
+        own.wait()
+        await_arrivals(shares.at[pl.ds(0, 16 * (BANDS - 1))], recv_sem.at[0])
+        spread = shares[...].astype(jnp.float32).reshape(BANDS, 2, 8, 128)
+        halves = [spread[:, half].reshape(FULL, 128) for half in range(2)]
+        both = jnp.concatenate(halves, axis=1).astype(jnp.bfloat16)
+        share_ref[...] = both
+        local = lax.dot_general(
+            both, both, (((1,), (1,)), ((), ())), preferred_element_type=jnp.float32
+        )
+        partial[...] = local.astype(jnp.bfloat16)
+
+        def send_piece(step, carry):
+            other = (place + step) % PLACES
+            at = pl.multiple_of(other * 16, 16)
+            remote(
+                partial.at[pl.ds(at, 16)], pieces.at[place], 1, place_of(other)
+            ).start()
+            return carry
+
+        lax.fori_loop(1, PLACES, send_piece, 0)
+        at = pl.multiple_of(place * 16, 16)
+        pieces[place] = partial[pl.ds(at, 16)]
+        await_arrivals(pieces.at[pl.ds(0, PLACES - 1)], recv_sem.at[1])
+        summed = jnp.sum(pieces[...].astype(jnp.float32), axis=0)
+        halved = jnp.concatenate([summed[:, :128], summed[:, 128:]], axis=0)
+        piece[...] = halved.reshape(BANDS, 1, 128)
+
+        def send_row(step, carry):
+            other = (band + step) % BANDS
+            remote(
+                piece.at[other], rows.at[band_share(band)], 2, {"band": other}
+            ).start()
+            return carry
+
+        lax.fori_loop(1, BANDS, send_row, 0)
+        rows[band_share(band)] = piece[band]
+        await_arrivals(rows.at[pl.ds(0, OWNERS - 1)], recv_sem.at[2])
+
+    @pl.when(jnp.logical_not(owns))
+    def _():
+        share_ref[...] = jnp.zeros_like(share_ref)
+        await_arrivals(rows, recv_sem.at[2])
+
+    total[...] = jnp.sum(rows[...], axis=0) / cells
+
+    def send_total(step, carry):
+        other = (band + step) % BANDS
+        remote(total, strips.at[band], 3, {"band": other}).start()
+        return carry
+
+    lax.fori_loop(1, BANDS, send_total, 0)
+    strips[band] = total[...]
+    await_arrivals(strips.at[pl.ds(0, BANDS - 1)], recv_sem.at[3])
+    strip[...] = strips[...].reshape(BANDS, 128)
+
+    def send_strip(step, carry):
+        other = (place + step) % PLACES
+        remote(strip, blocks.at[place], 4, place_of(other)).start()
+        return carry
+
+    lax.fori_loop(1, PLACES, send_strip, 0)
+    blocks[place] = strip[...]
+    await_arrivals(blocks.at[pl.ds(0, PLACES - 1)], recv_sem.at[4])
+    found = blocks[...]
+    gram_ref[:, :128] = found[:, :16].reshape(FULL, 128)
+    gram_ref[:, 128:] = found[:, 16:].reshape(FULL, 128)
+
+    @pl.when(owns)
+    def _():
+        await_arrivals(mine_ref.at[pl.ds(0, 16 * (OWNERS - 1))], send_sem.at[0])
+        await_arrivals(pieces.at[pl.ds(0, PLACES - 1)], send_sem.at[1])
+        await_arrivals(piece.at[pl.ds(0, BANDS - 1)], send_sem.at[2])
+
+    @pl.when(jnp.logical_not(owns))
+    def _():
+        await_arrivals(mine_ref, send_sem.at[0])
+
+    await_arrivals(strips.at[pl.ds(0, BANDS - 1)], send_sem.at[3])
+    await_arrivals(blocks.at[pl.ds(0, PLACES - 1)], send_sem.at[4])
+
+
+def gather_gram(mine, cells):
+    return pl.pallas_call(
+        functools.partial(gram_kernel, cells),
+        out_shape=(
+            jax.ShapeDtypeStruct((FULL, FULL), jnp.float32),
+            jax.ShapeDtypeStruct((FULL, FULL), jnp.bfloat16),
+        ),
+        in_specs=[pl.BlockSpec(memory_space=pltpu.VMEM)],
+        out_specs=(pl.BlockSpec(memory_space=pltpu.VMEM),) * 2,
+        scratch_shapes=[
+            pltpu.VMEM((BANDS * 16, 128), jnp.bfloat16),
+            pltpu.VMEM((FULL, FULL), jnp.bfloat16),
+            pltpu.VMEM((PLACES, 16, FULL), jnp.bfloat16),
+            pltpu.VMEM((BANDS, 1, 128), jnp.float32),
+            pltpu.VMEM((OWNERS, 1, 128), jnp.float32),
+            pltpu.VMEM((1, 128), jnp.float32),
+            pltpu.VMEM((BANDS, 1, 128), jnp.float32),
+            pltpu.VMEM((BANDS, 128), jnp.float32),
+            pltpu.VMEM((PLACES, BANDS, 128), jnp.float32),
+            pltpu.SemaphoreType.DMA((5,)),
+            pltpu.SemaphoreType.DMA((5,)),
+            pltpu.SemaphoreType.DMA,
+        ],
+        compiler_params=pltpu.CompilerParams(collective_id=1, has_side_effects=True),
+        name="gram_exchange",
+    )(mine)
+
+
+def rotate_kernel(coeffs_ref, share_ref, out_ref, parcels, arrived, send_sem, recv_sem, local_sem):
+    band = lax.axis_index("band")
+    owns = band % 4 != 3
+    barrier = pltpu.get_barrier_semaphore()
+
+    def greet_band(step, carry):
+        pl.semaphore_signal(
+            barrier, 1, device_id={"band": (band + step) % BANDS}, device_id_type=MESH
+        )
+        return carry
+
+    lax.fori_loop(1, BANDS, greet_band, 0)
+
+    @pl.when(owns)
+    def _():
+        turned = lax.dot_general(
+            coeffs_ref[...],
+            share_ref[...],
+            (((0,), (0,)), ((), ())),
+            preferred_element_type=jnp.float32,
+        )
+        halves = [turned[:, 128 * h : 128 * h + 128].reshape(BANDS, 1, 8, 128) for h in range(2)]
+        parcels[...] = (
+            jnp.concatenate(halves, axis=1).reshape(BANDS * 16, 128).astype(jnp.bfloat16)
+        )
+
+    pl.semaphore_wait(barrier, BANDS - 1)
+
+    @pl.when(owns)
+    def _():
+        to = pl.multiple_of(band_share(band) * 16, 16)
+
+        def send_parcel(step, carry):
+            other = (band + step) % BANDS
+            at = pl.multiple_of(other * 16, 16)
+            pltpu.make_async_remote_copy(
+                src_ref=parcels.at[pl.ds(at, 16)],
+                dst_ref=arrived.at[pl.ds(to, 16)],
+                send_sem=send_sem,
+                recv_sem=recv_sem,
+                device_id={"band": other},
+                device_id_type=MESH,
+            ).start()
+            return carry
+
+        lax.fori_loop(1, BANDS, send_parcel, 0)
+        at = pl.multiple_of(band * 16, 16)
+        own = pltpu.make_async_copy(
+            parcels.at[pl.ds(at, 16)], arrived.at[pl.ds(to, 16)], local_sem
+        )
+        own.start()
+        own.wait()
+        await_arrivals(arrived.at[pl.ds(0, 16 * (OWNERS - 1))], recv_sem)
+
+    @pl.when(jnp.logical_not(owns))
+    def _():
+        await_arrivals(arrived, recv_sem)
+
+    found = arrived[...].astype(jnp.float32).reshape(6, 8, 8, 128)
+    for at in range(6):
+        out_ref[:, at] = jnp.swapaxes(found[at], 0, 1)
+
+    @pl.when(owns)
+    def _():
+        await_arrivals(parcels.at[pl.ds(0, 16 * (BANDS - 1))], send_sem)
+
+
+def rotate(coeffs, share):
+    return pl.pallas_call(
+        rotate_kernel,
+        out_shape=jax.ShapeDtypeStruct((8, 6, 8, 128), jnp.float32),
+        in_specs=[pl.BlockSpec(memory_space=pltpu.VMEM)] * 2,
+        out_specs=pl.BlockSpec(memory_space=pltpu.VMEM),
+        scratch_shapes=[
+            pltpu.VMEM((BANDS * 16, 128), jnp.bfloat16),
+            pltpu.VMEM((OWNERS * 16, 128), jnp.bfloat16),
+            pltpu.SemaphoreType.DMA,
+            pltpu.SemaphoreType.DMA,
+            pltpu.SemaphoreType.DMA,
+        ],
+        compiler_params=pltpu.CompilerParams(collective_id=2, has_side_effects=True),
+        name="rotation_exchange",
+    )(coeffs, share)
+
+
 def body(orbitals, potential):
     half, center, sigma, sigma_two = filter_scalars()
     first = sigma / half * (apply_ham(orbitals, potential) - center * orbitals)
@@ -75,23 +370,13 @@
         - sigma * sigma_two * orbitals
     )
     local_count = orbitals.shape[0]
-    mine = second.astype(jnp.bfloat16).reshape(local_count, -1)
-    total_cells = mine.shape[1] * lax.axis_size("gx") * lax.axis_size("gy")
-    shares = lax.all_to_all(mine, "band", split_axis=1, concat_axis=0, tiled=True)
-    partial_gram = lax.dot_general(
-        shares, shares, (((1,), (1,)), ((), ())), preferred_element_type=jnp.float32
-    )
-    summed = lax.psum(partial_gram, ("band", "gx", "gy"))
-    gram = summed / total_cells
+    mine = second.astype(jnp.bfloat16).transpose(1, 2, 0, 3).reshape(-1, 128)
+    total_cells = mine.shape[0] * 16 * lax.axis_size("gx") * lax.axis_size("gy")
+    gram, share = gather_gram(mine, float(total_cells))
     coeffs = finish_coeffs(gram)
-    rotated_share = lax.dot_general(
-        coeffs, shares, (((0,), (0,)), ((), ())), preferred_element_type=jnp.float32
-    )
-    rotated = lax.all_to_all(
-        rotated_share.astype(jnp.bfloat16), "band", split_axis=0, concat_axis=1, tiled=True
-    ).astype(rotated_share.dtype)
+    rotated = rotate(coeffs, share)
     gram_rows = lax.dynamic_slice_in_dim(gram, lax.axis_index("band") * local_count, local_count, 0)
-    return (rotated.reshape(orbitals.shape), gram_rows)
+    return (rotated, gram_rows)
 
 
 def solution(mesh):

time: 656 us -> 203 us (0.31)
  waiting for transfers between devices: 506 us -> 35.4 us
  Pallas kernels: 0 us -> 71.7 us
  blocking collectives: 32.4 us -> 0 us
  between operations: 15.8 us -> 2.43 us
  starting transfers between devices: 26.2 us -> 16.6 us
    psum x1 -> x0, waiting for transfers between devices: 451 us -> none  [body(): summed = lax.psum(partial_gram, ('band', 'gx', 'gy'))]
    pallas_call x0 -> x2, Pallas kernels: none -> 71.7 us  [the longest x1 53.8 us: gather_gram(): pl.pallas_call(functools.partial(gram_kernel, cells), out_shape=(jax.Shap...]
    all_to_all x1 -> x0, blocking collectives: 32.4 us -> none  [body(): lax.all_to_all(mine, 'band', split_axis=1, concat_axis=0, tiled=True)]
    all_to_all x1 -> x0, waiting for transfers between devices: 16 us -> none  [body(): lax.all_to_all(rotated_share.astype(jnp.bfloat16), 'band', split_axis=0,...]
    all_to_all x1 -> x0, starting transfers between devices: 9.83 us -> none  [body(): lax.all_to_all(rotated_share.astype(jnp.bfloat16), 'band', split_axis=0,...]
  transfers between devices with their start and end apart: 10 -> 8, of which waited for: 9 -> 6; matrix products, arithmetic and copies ran while one was open for 1% -> 3% of each run, Pallas kernels for 0% -> 0%
where the time goes in v1:
time: 203 us; the launch traced here: 202 us
  Pallas kernels  71.7 us (35%)
  other arithmetic  58.8 us (29%)
  waiting for transfers between devices  35.4 us (17%)
  starting transfers between devices  16.6 us (8%)
  local copies, waits for them, and re-layouts  15.7 us (8%)
  between operations  2.43 us (1%)
    pallas_call x1, Pallas kernels, gather_gram(): pl.pallas_call(functools.partial(gram_kernel, cells), out_shape=(jax.Shap...  53.8 us
    another operation x6, other arithmetic, finish_coeffs(): lower = jnp.linalg.cholesky(gram)  34 us
    another operation x3, other arithmetic, finish_coeffs(): jax.scipy.linalg.solve_triangular(lower, jnp.eye(count, dtype=jnp.float32...  20.5 us
    ppermute x4, waiting for transfers between devices, extended(): after = lax.ppermute(leading, axis, down)  19.8 us
    pallas_call x1, Pallas kernels, rotate(): pl.pallas_call(rotate_kernel, out_shape=jax.ShapeDtypeStruct((8, 6, 8, 12...  17.9 us
    ppermute x4, waiting for transfers between devices, extended(): before = lax.ppermute(last, axis, up)  15.6 us
    ppermute x4, starting transfers between devices, extended(): after = lax.ppermute(leading, axis, down)  10.2 us
    ppermute x4, starting transfers between devices, extended(): before = lax.ppermute(last, axis, up)  6.4 us
  transfers between devices with their start and end apart: 8, of which 6 were waited for; matrix products, arithmetic and copies ran while one was open for 3% of the time, Pallas kernels for 0%

profile of v1, /device:TPU:24, one launch (start us, length us, event | category | flops | bytes accessed | tf_op | source)
XLA Modules:
  0.0 202.0 jit_solution(8016259103917121651)
XLA Ops:
  0.6 1.0 copy.8
  1.6 2.9 %collective-permute-start = (f32[8,6,8,128]{3,0,2,1:T(8,128)S(1)}, f32[8,6,8,128]{3,0,2,1:T(8,128)S(1)}, u32[]{:S(2)}, u32[]{:S(2)}) collective-permute-start(f32[8,6,8,128]{3,0,2,1:T(8,128)S(1)} %copy.8), channel_id=1, source_target_pairs={{2,0},{4,2},{6,4},{8,6},{10,8},{12,10},{14,12},{0,14},{3,1},{5,3},... | collective-permute-start | bytes 589832 | tf_op jit(solution)/shard_map/ppermute | solution.py:33
  5.4 0.8 fusion.135
  6.2 0.8 fusion.136
  7.0 0.8 fusion.137
  8.7 0.9 copy-done
  9.8 2.8 %collective-permute-start.2 = (f32[8,18,6,128]{3,0,2,1:T(8,128)S(1)}, f32[8,18,6,128]{3,0,2,1:T(8,128)S(1)}, u32[]{:S(2)}, u32[]{:S(2)}) collective-permute-start(f32[8,18,6,128]{3,0,2,1:T(8,128)S(1)} %get-tuple-element.30), channel_id=1, source_target_pairs={{1,0},{0,1},{3,2},{2,3},{5,4},{4,5},{7,6},{6,7},{9,8},{8,9},{11,10... | collective-permute-start | bytes 1327112 | tf_op jit(solution)/shard_map/ppermute | solution.py:33
  12.6 3.2 %collective-permute-start.3 = (f32[8,18,6,128]{3,0,2,1:T(8,128)S(1)}, f32[8,18,6,128]{3,0,2,1:T(8,128)S(1)}, u32[]{:S(2)}, u32[]{:S(2)}) collective-permute-start(f32[8,18,6,128]{3,0,2,1:T(8,128)S(1)} %get-tuple-element.31), channel_id=1, source_target_pairs={{0,1},{1,0},{2,3},{3,2},{4,5},{5,4},{6,7},{7,6},{8,9},{9,8},{10,11... | collective-permute-start | bytes 1327112 | tf_op jit(solution)/shard_map/ppermute | solution.py:32
  16.0 9.0 %collective-permute-done.2 = f32[8,18,6,128]{3,0,2,1:T(8,128)S(1)} collective-permute-done((f32[8,18,6,128]{3,0,2,1:T(8,128)S(1)}, f32[8,18,6,128]{3,0,2,1:T(8,128)S(1)}, u32[]{:S(2)}, u32[]{:S(2)}) %collective-permute-start.2) | collective-permute-done | bytes 442400 | tf_op jit(solution)/shard_map/ppermute | solution.py:33
  24.9 7.1 %collective-permute-done.3 = f32[8,18,6,128]{3,0,2,1:T(8,128)S(1)} collective-permute-done((f32[8,18,6,128]{3,0,2,1:T(8,128)S(1)}, f32[8,18,6,128]{3,0,2,1:T(8,128)S(1)}, u32[]{:S(2)}, u32[]{:S(2)}) %collective-permute-start.3) | collective-permute-done | bytes 442400 | tf_op jit(solution)/shard_map/ppermute | solution.py:32
  32.1 1.0 broadcast_multiply_fusion
  33.1 1.8 collective-permute-start.4
  36.2 2.0 collective-permute-done.4
  38.1 3.1 %collective-permute-done.5 = f32[8,6,8,128]{3,0,2,1:T(8,128)S(1)} collective-permute-done((f32[8,6,8,128]{3,0,2,1:T(8,128)S(1)}, f32[8,6,8,128]{3,0,2,1:T(8,128)S(1)}, u32[]{:S(2)}, u32[]{:S(2)}) %collective-permute-start.5) | collective-permute-done | bytes 196640 | tf_op jit(solution)/shard_map/ppermute | solution.py:32
  41.4 2.7 %collective-permute-start.6 = (f32[8,18,6,128]{3,0,2,1:T(8,128)S(1)}, f32[8,18,6,128]{3,0,2,1:T(8,128)S(1)}, u32[]{:S(2)}, u32[]{:S(2)}) collective-permute-start(f32[8,18,6,128]{3,0,2,1:T(8,128)S(1)} %get-tuple-element.28), channel_id=1, source_target_pairs={{1,0},{0,1},{3,2},{2,3},{5,4},{4,5},{7,6},{6,7},{9,8},{8,9},{11,10... | collective-permute-start | bytes 1327112 | tf_op jit(solution)/shard_map/ppermute | solution.py:33
  44.0 3.2 %collective-permute-start.7 = (f32[8,18,6,128]{3,0,2,1:T(8,128)S(1)}, f32[8,18,6,128]{3,0,2,1:T(8,128)S(1)}, u32[]{:S(2)}, u32[]{:S(2)}) collective-permute-start(f32[8,18,6,128]{3,0,2,1:T(8,128)S(1)} %get-tuple-element.29), channel_id=1, source_target_pairs={{0,1},{1,0},{2,3},{3,2},{4,5},{5,4},{6,7},{7,6},{8,9},{9,8},{10,11... | collective-permute-start | bytes 1327112 | tf_op jit(solution)/shard_map/ppermute | solution.py:32
  47.5 8.9 %collective-permute-done.6 = f32[8,18,6,128]{3,0,2,1:T(8,128)S(1)} collective-permute-done((f32[8,18,6,128]{3,0,2,1:T(8,128)S(1)}, f32[8,18,6,128]{3,0,2,1:T(8,128)S(1)}, u32[]{:S(2)}, u32[]{:S(2)}) %collective-permute-start.6) | collective-permute-done | bytes 442400 | tf_op jit(solution)/shard_map/ppermute | solution.py:33
  56.4 5.3 %collective-permute-done.7 = f32[8,18,6,128]{3,0,2,1:T(8,128)S(1)} collective-permute-done((f32[8,18,6,128]{3,0,2,1:T(8,128)S(1)}, f32[8,18,6,128]{3,0,2,1:T(8,128)S(1)}, u32[]{:S(2)}, u32[]{:S(2)}) %collective-permute-start.7) | collective-permute-done | bytes 442400 | tf_op jit(solution)/shard_map/ppermute | solution.py:32
  61.8 1.7 subtract_convert_fusion
  63.5 53.8 %gram_exchange.1 = (f32[256,256]{1,0:T(8,128)}, bf16[256,256]{1,0:T(8,128)(2,1)}) custom-call(bf16[384,128]{1,0:T(8,128)(2,1)} %bitcast.36), custom_call_target="tpu_custom_call" | custom-call | tf_op jit(solution)/shard_map/gram_exchange/pallas_call | solution.py:253
  117.3 1.1 copy.41
  118.6 11.7 %cholesky.50 = f32[128,128]{1,0:T(8,128)S(1)} custom-call(f32[128,128]{1,0:T(8,128)S(1)} %cholesky.118), custom_call_target="Cholesky" | custom-call | tf_op jit(solution)/shard_map/jit(cholesky)/cholesky | solution.py:67
  130.3 9.8 %custom-call.15 = f32[1,128,128]{1,2,0:T(8,128)S(1)} custom-call(f32[1,128,128]{2,1,0:T(8,128)S(1)} %get-tuple-element.90), custom_call_target="InvertDiagBlocksLowerTriangular" | custom-call | tf_op jit(solution)/shard_map/jit(cholesky)/cholesky | solution.py:67
  140.6 11.7 %cholesky.105 = f32[128,128]{1,0:T(8,128)S(1)} custom-call(f32[128,128]{1,0:T(8,128)S(1)} %convolution_subtract_fusion.1), custom_call_target="Cholesky" | custom-call | tf_op jit(solution)/shard_map/jit(cholesky)/cholesky | solution.py:67
  152.4 0.7 compare_reduce_fusion
  154.5 5.2 %while.1 = (s32[]{:T(128)}, f32[256,256]{1,0:T(8,128)S(1)}, s32[2,2]{1,0:T(2,128)S(1)}, f32[2,128,128]{2,1,0:T(8,128)}, s32[]{:T(128)}) while((s32[]{:T(128)}, f32[256,256]{1,0:T(8,128)S(1)}, s32[2,2]{1,0:T(2,128)S(1)}, f32[2,128,128]{2,1,0:T(8,128)}, s32[]{:T(128)}) %tuple.59), condition=%wide.while_cond, body=%wide.while_body.sunk | while | flops 2 | bytes 132705 | solution.py:68
  155.0 2.0 bitcast_dynamic-update-slice_fusion.2
  157.6 2.0 bitcast_dynamic-update-slice_fusion.2
  159.6 20.5 %custom-call.16 = f32[2,128,128]{1,2,0:T(8,128)S(1)} custom-call(f32[2,128,128]{2,1,0:T(8,128)} %get-tuple-element.13), custom_call_target="InvertDiagBlocksLowerTriangular" | custom-call | tf_op jit(solution)/shard_map/jit(_solve_triangular)/triangular_solve | solution.py:68
  181.2 0.7 maximum_bitcast_fusion.coeffs_ref
  181.8 17.9 %rotation_exchange.1 = f32[8,6,8,128]{3,2,1,0:T(8,128)} custom-call(bf16[256,256]{1,0:T(8,128)(2,1)} %maximum_bitcast_fusion.coeffs_ref, bf16[256,256]{1,0:T(8,128)(2,1)} %get-tuple-element.5.share_ref), custom_call_target="tpu_custom_call" | custom-call | tf_op jit(solution)/shard_map/rotation_exchange/pallas_call | solution.py:348
  200.4 1.6 copy.67
  (71 shorter events, 7.1 us)
Async XLA Ops:
  1.6 7.0 %collective-permute-start.1 = (f32[8,6,8,128]{3,0,2,1:T(8,128)S(1)}, f32[8,6,8,128]{3,0,2,1:T(8,128)S(1)}, u32[]{:S(2)}, u32[]{:S(2)}) collective-permute-start(f32[8,6,8,128]{3,0,2,1:T(8,128)S(1)} %copy.8), channel_id=1, source_target_pairs={{0,2},{2,4},{4,6},{6,8},{8,10},{10,12},{12,14},{14,0},{1,3},{3,5},... | collective-permute-start | bytes 589832 | tf_op jit(solution)/shard_map/ppermute | solution.py:32
  1.6 8.0 %collective-permute-start = (f32[8,6,8,128]{3,0,2,1:T(8,128)S(1)}, f32[8,6,8,128]{3,0,2,1:T(8,128)S(1)}, u32[]{:S(2)}, u32[]{:S(2)}) collective-permute-start(f32[8,6,8,128]{3,0,2,1:T(8,128)S(1)} %copy.8), channel_id=1, source_target_pairs={{2,0},{4,2},{6,4},{8,6},{10,8},{12,10},{14,12},{0,14},{3,1},{5,3},... | collective-permute-start | bytes 589832 | tf_op jit(solution)/shard_map/ppermute | solution.py:33
  8.6 0.9 copy-start
  9.7 6.1 %copy-start.8 = (f32[6,8,128]{2,1,0:T(8,128)S(1)}, f32[6,8,128]{2,1,0:T(8,128)}, u32[]{:S(2)}) copy-start(f32[6,8,128]{2,1,0:T(8,128)} %param.3) | copy-start | bytes 73732
  9.7 22.3 %copy-start.6 = (f32[8,6,8,123]{3,0,2,1:T(8,128)S(1)}, f32[8,6,8,123]{3,0,2,1:T(8,128)}, u32[]{:S(2)}) copy-start(f32[8,6,8,123]{3,0,2,1:T(8,128)} %get-tuple-element.82) | copy-start | bytes 566788
  9.8 15.1 %collective-permute-start.2 = (f32[8,18,6,128]{3,0,2,1:T(8,128)S(1)}, f32[8,18,6,128]{3,0,2,1:T(8,128)S(1)}, u32[]{:S(2)}, u32[]{:S(2)}) collective-permute-start(f32[8,18,6,128]{3,0,2,1:T(8,128)S(1)} %get-tuple-element.30), channel_id=1, source_target_pairs={{1,0},{0,1},{3,2},{2,3},{5,4},{4,5},{7,6},{6,7},{9,8},{8,9},{11,10... | collective-permute-start | bytes 1327112 | tf_op jit(solution)/shard_map/ppermute | solution.py:33
  12.6 19.5 %collective-permute-start.3 = (f32[8,18,6,128]{3,0,2,1:T(8,128)S(1)}, f32[8,18,6,128]{3,0,2,1:T(8,128)S(1)}, u32[]{:S(2)}, u32[]{:S(2)}) collective-permute-start(f32[8,18,6,128]{3,0,2,1:T(8,128)S(1)} %get-tuple-element.31), channel_id=1, source_target_pairs={{0,1},{1,0},{2,3},{3,2},{4,5},{5,4},{6,7},{7,6},{8,9},{9,8},{10,11... | collective-permute-start | bytes 1327112 | tf_op jit(solution)/shard_map/ppermute | solution.py:32
  15.8 16.2 %copy-start.2 = (f32[8,6,8,124]{3,0,2,1:T(8,128)S(1)}, f32[8,6,8,124]{3,0,2,1:T(8,128)}, u32[]{:S(2)}) copy-start(f32[8,6,8,124]{3,0,2,1:T(8,128)} %get-tuple-element.71) | copy-start | bytes 571396
  15.8 16.2 %copy-start.3 = (f32[8,6,8,5]{3,0,2,1:T(8,128)S(1)}, f32[8,6,8,5]{3,0,2,1:T(8,128)}, u32[]{:S(2)}) copy-start(f32[8,6,8,5]{3,0,2,1:T(8,128)} %get-tuple-element.79) | copy-start | bytes 23044
  15.8 16.2 %copy-start.4 = (f32[8,6,8,5]{3,0,2,1:T(8,128)S(1)}, f32[8,6,8,5]{3,0,2,1:T(8,128)}, u32[]{:S(2)}) copy-start(f32[8,6,8,5]{3,0,2,1:T(8,128)} %get-tuple-element.80) | copy-start | bytes 23044
  15.8 16.2 %copy-start.5 = (f32[8,6,8,123]{3,0,2,1:T(8,128)S(1)}, f32[8,6,8,123]{3,0,2,1:T(8,128)}, u32[]{:S(2)}) copy-start(f32[8,6,8,123]{3,0,2,1:T(8,128)} %get-tuple-element.81) | copy-start | bytes 566788
  33.1 5.0 %collective-permute-start.4 = (f32[8,6,8,128]{3,0,2,1:T(8,128)S(1)}, f32[8,6,8,128]{3,0,2,1:T(8,128)S(1)}, u32[]{:S(2)}, u32[]{:S(2)}) collective-permute-start(f32[8,6,8,128]{3,0,2,1:T(8,128)S(1)} %get-tuple-element.22), channel_id=1, source_target_pairs={{2,0},{4,2},{6,4},{8,6},{10,8},{12,10},{14,12},{0,14},{3,1},{5,3},... | collective-permute-start | bytes 589832 | tf_op jit(solution)/shard_map/ppermute | solution.py:33
  34.9 6.3 %collective-permute-start.5 = (f32[8,6,8,128]{3,0,2,1:T(8,128)S(1)}, f32[8,6,8,128]{3,0,2,1:T(8,128)S(1)}, u32[]{:S(2)}, u32[]{:S(2)}) collective-permute-start(f32[8,6,8,128]{3,0,2,1:T(8,128)S(1)} %get-tuple-element.22), channel_id=1, source_target_pairs={{0,2},{2,4},{4,6},{6,8},{8,10},{10,12},{12,14},{14,0},{1,3},{3,5},... | collective-permute-start | bytes 589832 | tf_op jit(solution)/shard_map/ppermute | solution.py:32
  41.4 15.0 %collective-permute-start.6 = (f32[8,18,6,128]{3,0,2,1:T(8,128)S(1)}, f32[8,18,6,128]{3,0,2,1:T(8,128)S(1)}, u32[]{:S(2)}, u32[]{:S(2)}) collective-permute-start(f32[8,18,6,128]{3,0,2,1:T(8,128)S(1)} %get-tuple-element.28), channel_id=1, source_target_pairs={{1,0},{0,1},{3,2},{2,3},{5,4},{4,5},{7,6},{6,7},{9,8},{8,9},{11,10... | collective-permute-start | bytes 1327112 | tf_op jit(solution)/shard_map/ppermute | solution.py:33
  44.0 17.6 %collective-permute-start.7 = (f32[8,18,6,128]{3,0,2,1:T(8,128)S(1)}, f32[8,18,6,128]{3,0,2,1:T(8,128)S(1)}, u32[]{:S(2)}, u32[]{:S(2)}) collective-permute-start(f32[8,18,6,128]{3,0,2,1:T(8,128)S(1)} %get-tuple-element.29), channel_id=1, source_target_pairs={{0,1},{1,0},{2,3},{3,2},{4,5},{5,4},{6,7},{7,6},{8,9},{9,8},{10,11... | collective-permute-start | bytes 1327112 | tf_op jit(solution)/shard_map/ppermute | solution.py:32
  117.3 1.2 copy-start.1
  154.4 25.7 %copy-start.7 = (pred[256,256]{1,0:T(32,128)(4,1)S(1)}, pred[256,256]{1,0:T(32,128)(4,1)}, u32[]{:S(2)}) copy-start(pred[256,256]{1,0:T(32,128)(4,1)} %iota_compare_fusion) | copy-start | bytes 196612

commit v2 on v1

--- a/solution.py
+++ b/solution.py
@@ -22,44 +22,12 @@
 bottom_edge = -6.5
 
 
-def extended(shard, sides, width):
-    for axis, dim in sides:
-        devices, length = (lax.axis_size(axis), shard.shape[dim])
-        up = [(i, (i + 1) % devices) for i in range(devices)]
-        down = [(j, i) for i, j in up]
-        last = lax.slice_in_dim(shard, length - width, length, axis=dim)
-        leading = lax.slice_in_dim(shard, 0, width, axis=dim)
-        before = lax.ppermute(last, axis, up)
-        after = lax.ppermute(leading, axis, down)
-        shard = jnp.concatenate([before, shard, after], axis=dim)
-    return shard
-
-
 def filter_scalars():
     half = (high_edge - low_edge) / 2.0
     center = (high_edge + low_edge) / 2.0
     sigma = half / (bottom_edge - center)
     sigma_two = 1.0 / (2.0 / sigma - sigma)
     return (half, center, sigma, sigma_two)
-
-
-def apply_ham(field, potential):
-    padded = extended(field, (("gx", 1), ("gy", 2)), 6)
-    size_x = field.shape[1]
-    size_y = field.shape[2]
-    laplace = 3.0 * stencil_coeffs[0] * field
-    for shift_by in range(1, 7):
-        coeff = stencil_coeffs[shift_by]
-        laplace = laplace + coeff * (
-            padded[:, 6 + shift_by : 6 + shift_by + size_x, 6 : 6 + size_y]
-            + padded[:, 6 - shift_by : 6 - shift_by + size_x, 6 : 6 + size_y]
-        )
-        laplace = laplace + coeff * (
-            padded[:, 6 : 6 + size_x, 6 + shift_by : 6 + shift_by + size_y]
-            + padded[:, 6 : 6 + size_x, 6 - shift_by : 6 - shift_by + size_y]
-        )
-        laplace = laplace + coeff * (jnp.roll(field, shift_by, 3) + jnp.roll(field, -shift_by, 3))
-    return -0.5 / spacing**2 * laplace + potential[None] * field
 
 
 def finish_coeffs(gram):
@@ -95,11 +63,31 @@
     pltpu.make_async_copy(buffer, buffer, sem).wait()
 
 
+def kinetic(wide, other, at):
+    own = wide[6 + at]
+    around = other[at]
+    column = jnp.concatenate([around, own, around], axis=0)
+    total = 3.0 * stencil_coeffs[0] * own
+    for m in range(1, 7):
+        near = wide[6 + at + m] + wide[6 + at - m]
+        near = near + (column[8 + m : 16 + m] + column[8 - m : 16 - m])
+        near = near + (pltpu.roll(own, m, 2) + pltpu.roll(own, 128 - m, 2))
+        total = total + stencil_coeffs[m] * near
+    return own, -0.5 / spacing**2 * total
+
+
 def gram_kernel(
     cells,
-    mine_ref,
+    orbitals_ref,
+    potential_ref,
     gram_ref,
     share_ref,
+    mine_ref,
+    outgoing,
+    halos,
+    base,
+    slope,
+    other_side,
     shares,
     partial,
     pieces,
@@ -109,6 +97,8 @@
     strips,
     strip,
     blocks,
+    halo_send,
+    halo_recv,
     send_sem,
     recv_sem,
     local_sem,
@@ -133,7 +123,75 @@
 
     lax.fori_loop(1, BANDS, greet_band, 0)
     lax.fori_loop(1, PLACES, greet_place, 0)
+
+    def turn(at, carry):
+        plane = jnp.swapaxes(orbitals_ref[:, at], 0, 1)
+        base[6 + at] = plane
+        rows_at = pl.ds(pl.multiple_of(at * 64, 64), 64)
+        outgoing[0, rows_at] = plane.reshape(64, 128).astype(jnp.bfloat16)
+        return carry
+
+    lax.fori_loop(0, 6, turn, 0)
     pl.semaphore_wait(barrier, BANDS - 1 + PLACES - 1)
+
+    place_x, place_y = lax.axis_index("gx"), lax.axis_index("gy")
+    sides = (
+        {"gx": (place_x + 1) % 8},
+        {"gx": (place_x + 7) % 8},
+        {"gy": 1 - place_y},
+    )
+
+    def halo_copy(turn_at, side):
+        return pltpu.make_async_remote_copy(
+            src_ref=outgoing.at[turn_at],
+            dst_ref=halos.at[turn_at, side],
+            send_sem=halo_send.at[turn_at, side],
+            recv_sem=halo_recv.at[turn_at, side],
+            device_id=sides[side],
+            device_id_type=MESH,
+        )
+
+    def halo_take(turn_at, wide):
+        for side in range(3):
+            halo_copy(turn_at, side).wait_recv()
+
+        def widen(at, carry):
+            rows_at = pl.ds(pl.multiple_of(at * 64, 64), 64)
+            for side, target, offset in ((0, wide, 0), (1, wide, 12), (2, other_side, 0)):
+                block = halos[turn_at, side, rows_at]
+                target[at + offset] = block.astype(jnp.float32).reshape(8, 8, 128)
+            return carry
+
+        lax.fori_loop(0, 6, widen, 0)
+
+    half, center, sigma, sigma_two = filter_scalars()
+    for side in (2, 0, 1):
+        halo_copy(0, side).start()
+    halo_take(0, base)
+
+    def first_step(at, carry):
+        own, moved = kinetic(base, other_side, at)
+        shifted = (potential_ref[at] - center)[:, None, :]
+        result = sigma / half * (moved + shifted * own)
+        slope[6 + at] = result
+        rows_at = pl.ds(pl.multiple_of(at * 64, 64), 64)
+        outgoing[1, rows_at] = result.reshape(64, 128).astype(jnp.bfloat16)
+        return carry
+
+    lax.fori_loop(0, 6, first_step, 0)
+    for side in (2, 0, 1):
+        halo_copy(1, side).start()
+    halo_take(1, slope)
+
+    def second_step(at, carry):
+        own, moved = kinetic(slope, other_side, at)
+        shifted = (potential_ref[at] - center)[:, None, :]
+        result = 2.0 * sigma_two / half * (moved + shifted * own) - sigma * sigma_two * base[6 + at]
+        rows_at = pl.ds(pl.multiple_of(at * 64, 64), 64)
+        mine_ref[rows_at] = result.reshape(64, 128).astype(jnp.bfloat16)
+        return carry
+
+    lax.fori_loop(0, 6, second_step, 0)
 
     def remote(source, target, phase, device):
         return pltpu.make_async_remote_copy(
@@ -245,20 +303,29 @@
     def _():
         await_arrivals(mine_ref, send_sem.at[0])
 
+    for turn_at in range(2):
+        for side in range(3):
+            halo_copy(turn_at, side).wait_send()
     await_arrivals(strips.at[pl.ds(0, BANDS - 1)], send_sem.at[3])
     await_arrivals(blocks.at[pl.ds(0, PLACES - 1)], send_sem.at[4])
 
 
-def gather_gram(mine, cells):
+def gather_gram(orbitals, potential, cells):
     return pl.pallas_call(
         functools.partial(gram_kernel, cells),
         out_shape=(
             jax.ShapeDtypeStruct((FULL, FULL), jnp.float32),
             jax.ShapeDtypeStruct((FULL, FULL), jnp.bfloat16),
         ),
-        in_specs=[pl.BlockSpec(memory_space=pltpu.VMEM)],
+        in_specs=[pl.BlockSpec(memory_space=pltpu.VMEM)] * 2,
         out_specs=(pl.BlockSpec(memory_space=pltpu.VMEM),) * 2,
         scratch_shapes=[
+            pltpu.VMEM((384, 128), jnp.bfloat16),
+            pltpu.VMEM((2, 384, 128), jnp.bfloat16),
+            pltpu.VMEM((2, 3, 384, 128), jnp.bfloat16),
+            pltpu.VMEM((18, 8, 8, 128), jnp.float32),
+            pltpu.VMEM((18, 8, 8, 128), jnp.float32),
+            pltpu.VMEM((6, 8, 8, 128), jnp.float32),
             pltpu.VMEM((BANDS * 16, 128), jnp.bfloat16),
             pltpu.VMEM((FULL, FULL), jnp.bfloat16),
             pltpu.VMEM((PLACES, 16, FULL), jnp.bfloat16),
@@ -268,13 +335,15 @@
             pltpu.VMEM((BANDS, 1, 128), jnp.float32),
             pltpu.VMEM((BANDS, 128), jnp.float32),
             pltpu.VMEM((PLACES, BANDS, 128), jnp.float32),
+            pltpu.SemaphoreType.DMA((2, 3)),
+            pltpu.SemaphoreType.DMA((2, 3)),
             pltpu.SemaphoreType.DMA((5,)),
             pltpu.SemaphoreType.DMA((5,)),
             pltpu.SemaphoreType.DMA,
         ],
         compiler_params=pltpu.CompilerParams(collective_id=1, has_side_effects=True),
         name="gram_exchange",
-    )(mine)
+    )(orbitals, potential)
 
 
 def rotate_kernel(coeffs_ref, share_ref, out_ref, parcels, arrived, send_sem, recv_sem, local_sem):
@@ -363,16 +432,10 @@
 
 
 def body(orbitals, potential):
-    half, center, sigma, sigma_two = filter_scalars()
-    first = sigma / half * (apply_ham(orbitals, potential) - center * orbitals)
-    second = (
-        2.0 * sigma_two / half * (apply_ham(first, potential) - center * first)
-        - sigma * sigma_two * orbitals
-    )
     local_count = orbitals.shape[0]
-    mine = second.astype(jnp.bfloat16).transpose(1, 2, 0, 3).reshape(-1, 128)
-    total_cells = mine.shape[0] * 16 * lax.axis_size("gx") * lax.axis_size("gy")
-    gram, share = gather_gram(mine, float(total_cells))
+    spots = orbitals.shape[1] * orbitals.shape[2] * orbitals.shape[3]
+    total_cells = spots * lax.axis_size("gx") * lax.axis_size("gy")
+    gram, share = gather_gram(orbitals, potential, float(total_cells))
     coeffs = finish_coeffs(gram)
     rotated = rotate(coeffs, share)
     gram_rows = lax.dynamic_slice_in_dim(gram, lax.axis_index("band") * local_count, local_count, 0)

time: 203 us -> 150 us (0.74)
  waiting for transfers between devices: 35.4 us -> 0 us
  starting transfers between devices: 16.6 us -> 0 us
  Pallas kernels: 71.7 us -> 81.6 us
  local copies, waits for them, and re-layouts: 15.7 us -> 8.3 us
  other arithmetic: 58.8 us -> 54.7 us
    ppermute x8 -> x0, waiting for transfers between devices: 35.4 us -> none  [the longest x4 19.8 us: extended(): after = lax.ppermute(leading, axis, down)]
    ppermute x8 -> x0, starting transfers between devices: 16.6 us -> none  [the longest x4 10.2 us: extended(): after = lax.ppermute(leading, axis, down)]
    pallas_call x1, Pallas kernels: 53.8 us -> 63.9 us  [gather_gram(): pl.pallas_call(functools.partial(gram_kernel, cells), out_shape=(jax.Shap...]
    slice x26 -> x0, local copies, waits for them, and re-layouts: 4.92 us -> none  [the longest x24 4.79 us: apply_ham(): jnp.roll(field, shift_by, 3) + jnp.roll(field, -shift_by, 3)]
  transfers between devices with their start and end apart: 8 -> 0, of which waited for: 6 -> 0; matrix products, arithmetic and copies ran while one was open for 3% -> 0% of each run, Pallas kernels for 0% -> 0%
where the time goes in v2:
time: 150 us; the launch traced here: 148 us
  Pallas kernels  81.6 us (54%)
  other arithmetic  54.7 us (36%)
  local copies, waits for them, and re-layouts  8.3 us (6%)
  between operations  2.04 us (1%)
    pallas_call x1, Pallas kernels, gather_gram(): pl.pallas_call(functools.partial(gram_kernel, cells), out_shape=(jax.Shap...  63.9 us
    another operation x6, other arithmetic, finish_coeffs(): lower = jnp.linalg.cholesky(gram)  34 us
    another operation x3, other arithmetic, finish_coeffs(): jax.scipy.linalg.solve_triangular(lower, jnp.eye(count, dtype=jnp.float32...  19.9 us
    pallas_call x1, Pallas kernels, rotate(): pl.pallas_call(rotate_kernel, out_shape=jax.ShapeDtypeStruct((8, 6, 8, 12...  17.8 us
    another operation x6, local copies, waits for them, and re-layouts  4.02 us

profile of v2, /device:TPU:24, one launch (start us, length us, event | category | flops | bytes accessed | tf_op | source)
XLA Modules:
  0.0 148.1 jit_solution(16081583434070955845)
XLA Ops:
  0.6 0.1 triangular_solve.63
  0.8 63.9 %gram_exchange.1 = (f32[256,256]{1,0:T(8,128)}, bf16[256,256]{1,0:T(8,128)(2,1)}) custom-call(f32[8,6,8,128]{3,2,1,0:T(8,128)} %orbitals_ref.1, f32[6,8,128]{2,1,0:T(8,128)} %potential_ref.1), custom_call_target="tpu_custom_call" | custom-call | tf_op jit(solution)/shard_map/gram_exchange/pallas_call | solution.py:314
  64.7 1.3 constant_dynamic-slice_fusion.1
  66.0 0.0 copy-start
  66.0 1.1 copy.4
  67.1 0.0 copy-done
  67.2 11.7 %cholesky.50 = f32[128,128]{1,0:T(8,128)S(1)} custom-call(f32[128,128]{1,0:T(8,128)S(1)} %cholesky.118), custom_call_target="Cholesky" | custom-call | tf_op jit(solution)/shard_map/jit(cholesky)/cholesky | solution.py:35
  78.9 9.8 %custom-call.15 = f32[1,128,128]{1,2,0:T(8,128)S(1)} custom-call(f32[1,128,128]{2,1,0:T(8,128)S(1)} %get-tuple-element.27), custom_call_target="InvertDiagBlocksLowerTriangular" | custom-call | tf_op jit(solution)/shard_map/jit(cholesky)/cholesky | solution.py:35
  88.8 0.2 constant_dynamic-update-slice_fusion
  89.0 0.3 convolution_subtract_fusion.1
  89.3 11.7 %cholesky.105 = f32[128,128]{1,0:T(8,128)S(1)} custom-call(f32[128,128]{1,0:T(8,128)S(1)} %convolution_subtract_fusion.1), custom_call_target="Cholesky" | custom-call | tf_op jit(solution)/shard_map/jit(cholesky)/cholesky | solution.py:35
  101.0 0.7 compare_reduce_fusion
  103.0 4.1 %while.1 = (s32[]{:T(128)}, f32[256,256]{1,0:T(8,128)S(1)}, s32[2,2]{1,0:T(2,128)S(1)}, f32[2,128,128]{2,1,0:T(8,128)S(1)}, s32[]{:T(128)}) while((s32[]{:T(128)}, f32[256,256]{1,0:T(8,128)S(1)}, s32[2,2]{1,0:T(2,128)S(1)}, f32[2,128,128]{2,1,0:T(8,128)S(1)}, s32[]{:T(128)}) %tuple.27), condition=%wide.while_cond, body=%wide.while_body.sunk | while | flops 2 | bytes 131189 | solution.py:36
  103.0 0.7 fusion.13
  103.7 1.3 bitcast_dynamic-update-slice_fusion.2
  105.1 0.7 fusion.13
  105.7 1.3 bitcast_dynamic-update-slice_fusion.2
  107.1 19.9 %custom-call.16 = f32[2,128,128]{1,2,0:T(8,128)S(1)} custom-call(f32[2,128,128]{2,1,0:T(8,128)S(1)} %get-tuple-element.13), custom_call_target="InvertDiagBlocksLowerTriangular" | custom-call | tf_op jit(solution)/shard_map/jit(_solve_triangular)/triangular_solve | solution.py:36
  127.0 0.3 fusion.1
  127.2 0.3 convolution_subtract_fusion
  127.5 0.4 convolution_convert_fusion
  127.9 0.1 copy.5
  128.0 0.7 maximum_bitcast_fusion.coeffs_ref
  128.7 17.8 %rotation_exchange.1 = f32[8,6,8,128]{3,2,1,0:T(8,128)} custom-call(bf16[256,256]{1,0:T(8,128)(2,1)} %maximum_bitcast_fusion.coeffs_ref, bf16[256,256]{1,0:T(8,128)(2,1)} %get-tuple-element.5.share_ref), custom_call_target="tpu_custom_call" | custom-call | tf_op jit(solution)/shard_map/rotation_exchange/pallas_call | solution.py:417
  146.5 1.6 %copy.20 = f32[8,6,8,128]{3,2,1,0:T(8,128)} copy(f32[8,6,8,128]{3,2,1,0:T(8,128)} %rotation_exchange.1) | data formatting | bytes 393216
  (11 shorter events, 0.2 us)
Async XLA Ops:
  66.0 1.2 copy-start

commit v3 on v2

--- a/solution.py
+++ b/solution.py
@@ -28,15 +28,6 @@
     sigma = half / (bottom_edge - center)
     sigma_two = 1.0 / (2.0 / sigma - sigma)
     return (half, center, sigma, sigma_two)
-
-
-def finish_coeffs(gram):
-    count = gram.shape[0]
-    lower = jnp.linalg.cholesky(gram)
-    inv_lower = jax.scipy.linalg.solve_triangular(
-        lower, jnp.eye(count, dtype=jnp.float32), lower=True
-    )
-    return inv_lower.T.astype(jnp.bfloat16)
 
 
 MESH = pl.DeviceIdType.MESH
@@ -346,7 +337,94 @@
     )(orbitals, potential)
 
 
-def rotate_kernel(coeffs_ref, share_ref, out_ref, parcels, arrived, send_sem, recv_sem, local_sem):
+def split_parts(value):
+    high = value.astype(jnp.bfloat16)
+    rest = value - high.astype(jnp.float32)
+    middle = rest.astype(jnp.bfloat16)
+    return high, middle, (rest - middle.astype(jnp.float32)).astype(jnp.bfloat16)
+
+
+def inverse_factor(matrix, rows_buf, cols_buf, panel_buf):
+    size = matrix.shape[1]
+    width = panel_buf.shape[0]
+    lane = lax.broadcasted_iota(jnp.int32, (1, size), 1)
+    done = []
+    for begin in range(0, size, width):
+        end = begin + width
+        head = matrix[:width]
+        rows_buf[...] = head
+        for j in range(width):
+            cols_buf[j] = jnp.broadcast_to(head[:, begin + j : begin + j + 1], (width, size))
+        entry = {}
+        for j in range(width):
+            for i in range(j, width):
+                entry[i, j] = cols_buf[j, i : i + 1, :]
+        inside = (lane >= begin) & (lane < end)
+        row = [
+            jnp.where(inside, (lane == begin + i).astype(jnp.float32), rows_buf[i : i + 1, :])
+            for i in range(width)
+        ]
+        for p in range(width):
+            scale = lax.rsqrt(entry[p, p])
+            for i in range(p + 1, width):
+                entry[i, p] = entry[i, p] * scale
+            lead = row[p] * scale
+            for i in range(p + 1, width):
+                for j in range(p + 1, i + 1):
+                    entry[i, j] = entry[i, j] - entry[i, p] * entry[j, p]
+                row[i] = row[i] - entry[i, p] * lead
+            panel_buf[p : p + 1, :] = lead
+        panel = panel_buf[...]
+        done.append(jnp.where(jnp.broadcast_to(lane < end, (width, size)), panel, 0.0))
+        if end < size:
+            high, middle, low = split_parts(panel)
+            update = lax.dot_general(
+                jnp.concatenate([high, high, middle, high, low, middle], axis=0),
+                jnp.concatenate([high, middle, high, low, high, middle], axis=0),
+                (((0,), (0,)), ((), ())),
+                preferred_element_type=jnp.float32,
+            )
+            rest = jnp.where(jnp.broadcast_to(inside, (size - end, size)), 0.0, matrix[width:])
+            matrix = rest - update[end:]
+    return jnp.concatenate(done, axis=0)
+
+
+def full_dot(left, right, left_dim, right_dim):
+    return lax.dot_general(
+        left,
+        right,
+        (((left_dim,), (right_dim,)), ((), ())),
+        preferred_element_type=jnp.float32,
+        precision=lax.Precision.HIGHEST,
+    )
+
+
+def fill_inverse(gram_ref, inverse_ref, buffers):
+    upper = inverse_factor(gram_ref[:128, :128], *buffers)
+    lower_left = full_dot(gram_ref[128:, :128], upper, 1, 1)
+    remaining = gram_ref[128:, 128:] - full_dot(lower_left, lower_left, 1, 1)
+    carried = full_dot(lower_left, upper, 1, 0)
+    lower = inverse_factor(remaining, *buffers)
+    inverse_ref[:128, :128] = upper.astype(jnp.bfloat16)
+    inverse_ref[:128, 128:] = jnp.zeros((128, 128), jnp.bfloat16)
+    inverse_ref[128:, 128:] = lower.astype(jnp.bfloat16)
+    inverse_ref[128:, :128] = (-full_dot(lower, carried, 1, 0)).astype(jnp.bfloat16)
+
+
+def rotate_kernel(
+    gram_ref,
+    share_ref,
+    out_ref,
+    inverse,
+    rows_buf,
+    cols_buf,
+    panel_buf,
+    parcels,
+    arrived,
+    send_sem,
+    recv_sem,
+    local_sem,
+):
     band = lax.axis_index("band")
     owns = band % 4 != 3
     barrier = pltpu.get_barrier_semaphore()
@@ -361,10 +439,11 @@
 
     @pl.when(owns)
     def _():
+        fill_inverse(gram_ref, inverse, (rows_buf, cols_buf, panel_buf))
         turned = lax.dot_general(
-            coeffs_ref[...],
+            inverse[...],
             share_ref[...],
-            (((0,), (0,)), ((), ())),
+            (((1,), (0,)), ((), ())),
             preferred_element_type=jnp.float32,
         )
         halves = [turned[:, 128 * h : 128 * h + 128].reshape(BANDS, 1, 8, 128) for h in range(2)]
@@ -413,13 +492,17 @@
         await_arrivals(parcels.at[pl.ds(0, 16 * (BANDS - 1))], send_sem)
 
 
-def rotate(coeffs, share):
+def rotate(gram, share):
     return pl.pallas_call(
         rotate_kernel,
         out_shape=jax.ShapeDtypeStruct((8, 6, 8, 128), jnp.float32),
         in_specs=[pl.BlockSpec(memory_space=pltpu.VMEM)] * 2,
         out_specs=pl.BlockSpec(memory_space=pltpu.VMEM),
         scratch_shapes=[
+            pltpu.VMEM((FULL, FULL), jnp.bfloat16),
+            pltpu.VMEM((16, 128), jnp.float32),
+            pltpu.VMEM((16, 16, 128), jnp.float32),
+            pltpu.VMEM((16, 128), jnp.float32),
             pltpu.VMEM((BANDS * 16, 128), jnp.bfloat16),
             pltpu.VMEM((OWNERS * 16, 128), jnp.bfloat16),
             pltpu.SemaphoreType.DMA,
@@ -428,7 +511,7 @@
         ],
         compiler_params=pltpu.CompilerParams(collective_id=2, has_side_effects=True),
         name="rotation_exchange",
-    )(coeffs, share)
+    )(gram, share)
 
 
 def body(orbitals, potential):
@@ -436,8 +519,7 @@
     spots = orbitals.shape[1] * orbitals.shape[2] * orbitals.shape[3]
     total_cells = spots * lax.axis_size("gx") * lax.axis_size("gy")
     gram, share = gather_gram(orbitals, potential, float(total_cells))
-    coeffs = finish_coeffs(gram)
-    rotated = rotate(coeffs, share)
+    rotated = rotate(gram, share)
     gram_rows = lax.dynamic_slice_in_dim(gram, lax.axis_index("band") * local_count, local_count, 0)
     return (rotated, gram_rows)
 

time: 150 us -> 92.7 us (0.62)
  the two profiles are of different devices: /device:TPU:24 before, /device:TPU:1 now
where the time goes in v3:
time: 92.7 us; the launch traced here: 92.4 us
  Pallas kernels  88.9 us (96%)
  local copies, waits for them, and re-layouts  2.92 us (3%)
    pallas_call x1, Pallas kernels, gather_gram(): pl.pallas_call(functools.partial(gram_kernel, cells), out_shape=(jax.Shap...  65.6 us
    pallas_call x1, Pallas kernels, rotate(): pl.pallas_call(rotate_kernel, out_shape=jax.ShapeDtypeStruct((8, 6, 8, 12...  23.3 us

profile of v3, /device:TPU:1, one launch (start us, length us, event | category | flops | bytes accessed | tf_op | source)
XLA Modules:
  0.0 92.4 jit_solution(13301760612756463546)
XLA Ops:
  0.6 65.6 %gram_exchange.1 = (f32[256,256]{1,0:T(8,128)}, bf16[256,256]{1,0:T(8,128)(2,1)}) custom-call(f32[8,6,8,128]{3,2,1,0:T(8,128)} %orbitals_ref.1, f32[6,8,128]{2,1,0:T(8,128)} %potential_ref.1), custom_call_target="tpu_custom_call" | custom-call | tf_op jit(solution)/shard_map/gram_exchange/pallas_call | solution.py:305
  66.3 1.3 %constant_dynamic-slice_fusion = f32[8,256]{1,0:T(8,128)} fusion(f32[256,256]{1,0:T(8,128)} %get-tuple-element.4.gram_ref, s32[]{:T(128)S(6)} %select_n.3), kind=kLoop, calls=%fused_computation | loop fusion | bytes 16388 | tf_op jit(solution)/shard_map/dynamic_slice | solution.py:523
  67.6 23.3 %rotation_exchange.1 = f32[8,6,8,128]{3,2,1,0:T(8,128)} custom-call(f32[256,256]{1,0:T(8,128)} %get-tuple-element.4.gram_ref, bf16[256,256]{1,0:T(8,128)(2,1)} %get-tuple-element.5.share_ref), custom_call_target="tpu_custom_call" | custom-call | tf_op jit(solution)/shard_map/rotation_exchange/pallas_call | solution.py:496
  90.8 1.6 %copy.5 = f32[8,6,8,128]{3,2,1,0:T(8,128)} copy(f32[8,6,8,128]{3,2,1,0:T(8,128)} %rotation_exchange.1) | data formatting | bytes 393216

commit v4 on v3

--- a/solution.py
+++ b/solution.py
@@ -33,8 +33,11 @@
 MESH = pl.DeviceIdType.MESH
 BANDS = 32
 OWNERS = 24
-PLACES = 16
-GRID_Y = 2
+LAYERS = 16
+SENDERS = 12
+PLANE = 32
+GRID_X = 8
+GRID_Y = 4
 FULL = 256
 
 
@@ -46,8 +49,28 @@
     return (band // 4) * 3 + band % 4
 
 
-def place_of(index):
-    return {"gx": index // GRID_Y, "gy": index % GRID_Y}
+def far_first(step, count):
+    reach = (step + 1) // 2
+    return count // 2 + reach * (2 * (step % 2) - 1)
+
+
+def band_partner(band, step):
+    side = (band // LAYERS + 1 + step) % 2
+    return side * LAYERS + (band % LAYERS + far_first(step // 2, LAYERS)) % LAYERS
+
+
+def layer_partner(band, step):
+    return (band // LAYERS) * LAYERS + (band % LAYERS + far_first(step, LAYERS)) % LAYERS
+
+
+def plane_partner(place, step):
+    across = (place // GRID_Y + far_first(step // GRID_Y, GRID_X)) % GRID_X
+    return across * GRID_Y + (place + far_first(step % GRID_Y, GRID_Y)) % GRID_Y
+
+
+def plane_device(place, layer):
+    row = place % GRID_Y
+    return {"band": (row // 2) * LAYERS + layer, "gx": place // GRID_Y, "gy": row % 2}
 
 
 def await_arrivals(buffer, sem):
@@ -83,10 +106,8 @@
     partial,
     pieces,
     piece,
-    rows,
+    layers,
     total,
-    strips,
-    strip,
     blocks,
     halo_send,
     halo_recv,
@@ -95,25 +116,31 @@
     local_sem,
 ):
     band = lax.axis_index("band")
-    place = lax.axis_index("gx") * GRID_Y + lax.axis_index("gy")
+    layer = band % LAYERS
+    place = lax.axis_index("gx") * GRID_Y + (band // LAYERS) * 2 + lax.axis_index("gy")
     owns = band % 4 != 3
 
     barrier = pltpu.get_barrier_semaphore()
 
+    def greet(device):
+        pl.semaphore_signal(barrier, 1, device_id=device, device_id_type=MESH)
+
     def greet_band(step, carry):
-        pl.semaphore_signal(
-            barrier, 1, device_id={"band": (band + step) % BANDS}, device_id_type=MESH
-        )
-        return carry
-
-    def greet_place(step, carry):
-        pl.semaphore_signal(
-            barrier, 1, device_id=place_of((place + step) % PLACES), device_id_type=MESH
-        )
-        return carry
-
-    lax.fori_loop(1, BANDS, greet_band, 0)
-    lax.fori_loop(1, PLACES, greet_place, 0)
+        greet({"band": band_partner(band, step)})
+        return carry
+
+    def greet_plane(step, carry):
+        other = plane_partner(place, step)
+        alike = (other // GRID_Y == lax.axis_index("gx")) & (other % 2 == lax.axis_index("gy"))
+
+        @pl.when(jnp.logical_not(alike))
+        def _():
+            greet(plane_device(other, layer))
+
+        return carry
+
+    lax.fori_loop(0, BANDS - 1, greet_band, 0)
+    lax.fori_loop(0, PLANE - 1, greet_plane, 0)
 
     def turn(at, carry):
         plane = jnp.swapaxes(orbitals_ref[:, at], 0, 1)
@@ -123,7 +150,7 @@
         return carry
 
     lax.fori_loop(0, 6, turn, 0)
-    pl.semaphore_wait(barrier, BANDS - 1 + PLACES - 1)
+    pl.semaphore_wait(barrier, BANDS - 1 + PLANE - 2)
 
     place_x, place_y = lax.axis_index("gx"), lax.axis_index("gy")
     sides = (
@@ -195,7 +222,7 @@
         )
 
     def cell_share(step, carry):
-        other = (band + step) % BANDS
+        other = band_partner(band, step)
 
         @pl.when(other % 4 != 3)
         def _():
@@ -207,7 +234,7 @@
 
         return carry
 
-    lax.fori_loop(1, BANDS, cell_share, 0)
+    lax.fori_loop(0, BANDS - 1, cell_share, 0)
 
     @pl.when(owns)
     def _():
@@ -226,69 +253,58 @@
         local = lax.dot_general(
             both, both, (((1,), (1,)), ((), ())), preferred_element_type=jnp.float32
         )
-        partial[...] = local.astype(jnp.bfloat16)
+        sides = [local[:, 128 * h : 128 * h + 128].reshape(PLANE, 1, 8, 128) for h in range(2)]
+        partial[...] = (
+            jnp.concatenate(sides, axis=1).reshape(PLANE, 16, 128).astype(jnp.bfloat16)
+        )
 
         def send_piece(step, carry):
-            other = (place + step) % PLACES
-            at = pl.multiple_of(other * 16, 16)
+            other = plane_partner(place, step)
             remote(
-                partial.at[pl.ds(at, 16)], pieces.at[place], 1, place_of(other)
+                partial.at[other], pieces.at[place], 1, plane_device(other, layer)
             ).start()
             return carry
 
-        lax.fori_loop(1, PLACES, send_piece, 0)
-        at = pl.multiple_of(place * 16, 16)
-        pieces[place] = partial[pl.ds(at, 16)]
-        await_arrivals(pieces.at[pl.ds(0, PLACES - 1)], recv_sem.at[1])
-        summed = jnp.sum(pieces[...].astype(jnp.float32), axis=0)
-        halved = jnp.concatenate([summed[:, :128], summed[:, 128:]], axis=0)
-        piece[...] = halved.reshape(BANDS, 1, 128)
-
-        def send_row(step, carry):
-            other = (band + step) % BANDS
+        lax.fori_loop(0, PLANE - 1, send_piece, 0)
+        pieces[place] = partial[place]
+        await_arrivals(pieces.at[pl.ds(0, PLANE - 1)], recv_sem.at[1])
+        piece[...] = jnp.sum(pieces[...].astype(jnp.float32), axis=0).astype(jnp.bfloat16)
+        at_layer = band_share(layer)
+
+        def send_layer(step, carry):
             remote(
-                piece.at[other], rows.at[band_share(band)], 2, {"band": other}
+                piece, layers.at[at_layer], 2, {"band": layer_partner(band, step)}
             ).start()
             return carry
 
-        lax.fori_loop(1, BANDS, send_row, 0)
-        rows[band_share(band)] = piece[band]
-        await_arrivals(rows.at[pl.ds(0, OWNERS - 1)], recv_sem.at[2])
+        lax.fori_loop(0, LAYERS - 1, send_layer, 0)
+        layers[at_layer] = piece[...]
+        await_arrivals(layers.at[pl.ds(0, SENDERS - 1)], recv_sem.at[2])
 
     @pl.when(jnp.logical_not(owns))
     def _():
         share_ref[...] = jnp.zeros_like(share_ref)
-        await_arrivals(rows, recv_sem.at[2])
-
-    total[...] = jnp.sum(rows[...], axis=0) / cells
+        await_arrivals(layers, recv_sem.at[2])
+
+    total[...] = jnp.sum(layers[...].astype(jnp.float32), axis=0) / cells
 
     def send_total(step, carry):
-        other = (band + step) % BANDS
-        remote(total, strips.at[band], 3, {"band": other}).start()
-        return carry
-
-    lax.fori_loop(1, BANDS, send_total, 0)
-    strips[band] = total[...]
-    await_arrivals(strips.at[pl.ds(0, BANDS - 1)], recv_sem.at[3])
-    strip[...] = strips[...].reshape(BANDS, 128)
-
-    def send_strip(step, carry):
-        other = (place + step) % PLACES
-        remote(strip, blocks.at[place], 4, place_of(other)).start()
-        return carry
-
-    lax.fori_loop(1, PLACES, send_strip, 0)
-    blocks[place] = strip[...]
-    await_arrivals(blocks.at[pl.ds(0, PLACES - 1)], recv_sem.at[4])
+        other = plane_partner(place, step)
+        remote(total, blocks.at[place], 3, plane_device(other, layer)).start()
+        return carry
+
+    lax.fori_loop(0, PLANE - 1, send_total, 0)
+    blocks[place] = total[...]
+    await_arrivals(blocks.at[pl.ds(0, PLANE - 1)], recv_sem.at[3])
     found = blocks[...]
-    gram_ref[:, :128] = found[:, :16].reshape(FULL, 128)
-    gram_ref[:, 128:] = found[:, 16:].reshape(FULL, 128)
+    gram_ref[:, :128] = found[:, :8].reshape(FULL, 128)
+    gram_ref[:, 128:] = found[:, 8:].reshape(FULL, 128)
 
     @pl.when(owns)
     def _():
         await_arrivals(mine_ref.at[pl.ds(0, 16 * (OWNERS - 1))], send_sem.at[0])
-        await_arrivals(pieces.at[pl.ds(0, PLACES - 1)], send_sem.at[1])
-        await_arrivals(piece.at[pl.ds(0, BANDS - 1)], send_sem.at[2])
+        await_arrivals(pieces.at[pl.ds(0, PLANE - 1)], send_sem.at[1])
+        await_arrivals(pieces.at[pl.ds(0, LAYERS - 1)], send_sem.at[2])
 
     @pl.when(jnp.logical_not(owns))
     def _():
@@ -297,8 +313,7 @@
     for turn_at in range(2):
         for side in range(3):
             halo_copy(turn_at, side).wait_send()
-    await_arrivals(strips.at[pl.ds(0, BANDS - 1)], send_sem.at[3])
-    await_arrivals(blocks.at[pl.ds(0, PLACES - 1)], send_sem.at[4])
+    await_arrivals(blocks.at[pl.ds(0, PLANE - 1)], send_sem.at[3])
 
 
 def gather_gram(orbitals, potential, cells):
@@ -318,18 +333,16 @@
             pltpu.VMEM((18, 8, 8, 128), jnp.float32),
             pltpu.VMEM((6, 8, 8, 128), jnp.float32),
             pltpu.VMEM((BANDS * 16, 128), jnp.bfloat16),
-            pltpu.VMEM((FULL, FULL), jnp.bfloat16),
-            pltpu.VMEM((PLACES, 16, FULL), jnp.bfloat16),
-            pltpu.VMEM((BANDS, 1, 128), jnp.float32),
-            pltpu.VMEM((OWNERS, 1, 128), jnp.float32),
-            pltpu.VMEM((1, 128), jnp.float32),
-            pltpu.VMEM((BANDS, 1, 128), jnp.float32),
-            pltpu.VMEM((BANDS, 128), jnp.float32),
-            pltpu.VMEM((PLACES, BANDS, 128), jnp.float32),
+            pltpu.VMEM((PLANE, 16, 128), jnp.bfloat16),
+            pltpu.VMEM((PLANE, 16, 128), jnp.bfloat16),
+            pltpu.VMEM((16, 128), jnp.bfloat16),
+            pltpu.VMEM((SENDERS, 16, 128), jnp.bfloat16),
+            pltpu.VMEM((16, 128), jnp.float32),
+            pltpu.VMEM((PLANE, 16, 128), jnp.float32),
             pltpu.SemaphoreType.DMA((2, 3)),
             pltpu.SemaphoreType.DMA((2, 3)),
-            pltpu.SemaphoreType.DMA((5,)),
-            pltpu.SemaphoreType.DMA((5,)),
+            pltpu.SemaphoreType.DMA((4,)),
+            pltpu.SemaphoreType.DMA((4,)),
             pltpu.SemaphoreType.DMA,
         ],
         compiler_params=pltpu.CompilerParams(collective_id=1, has_side_effects=True),
@@ -431,11 +444,11 @@
 
     def greet_band(step, carry):
         pl.semaphore_signal(
-            barrier, 1, device_id={"band": (band + step) % BANDS}, device_id_type=MESH
-        )
-        return carry
-
-    lax.fori_loop(1, BANDS, greet_band, 0)
+            barrier, 1, device_id={"band": band_partner(band, step)}, device_id_type=MESH
+        )
+        return carry
+
+    lax.fori_loop(0, BANDS - 1, greet_band, 0)
 
     @pl.when(owns)
     def _():
@@ -458,7 +471,7 @@
         to = pl.multiple_of(band_share(band) * 16, 16)
 
         def send_parcel(step, carry):
-            other = (band + step) % BANDS
+            other = band_partner(band, step)
             at = pl.multiple_of(other * 16, 16)
             pltpu.make_async_remote_copy(
                 src_ref=parcels.at[pl.ds(at, 16)],
@@ -470,7 +483,7 @@
             ).start()
             return carry
 
-        lax.fori_loop(1, BANDS, send_parcel, 0)
+        lax.fori_loop(0, BANDS - 1, send_parcel, 0)
         at = pl.multiple_of(band * 16, 16)
         own = pltpu.make_async_copy(
             parcels.at[pl.ds(at, 16)], arrived.at[pl.ds(to, 16)], local_sem

time: 92.7 us -> 82.9 us (0.89)
  the two profiles are of different devices: /device:TPU:1 before, /device:TPU:2 now
where the time goes in v4:
time: 82.9 us; the launch traced here: 82.7 us
  Pallas kernels  79.1 us (95%)
  local copies, waits for them, and re-layouts  2.92 us (4%)
    pallas_call x1, Pallas kernels, gather_gram(): pl.pallas_call(functools.partial(gram_kernel, cells), out_shape=(jax.Shap...  57.5 us
    pallas_call x1, Pallas kernels, rotate(): pl.pallas_call(rotate_kernel, out_shape=jax.ShapeDtypeStruct((8, 6, 8, 12...  21.7 us

profile of v4, /device:TPU:2, one launch (start us, length us, event | category | flops | bytes accessed | tf_op | source)
XLA Modules:
  0.0 82.7 jit_solution(17395896990259716670)
XLA Ops:
  0.6 57.5 %gram_exchange.1 = (f32[256,256]{1,0:T(8,128)}, bf16[256,256]{1,0:T(8,128)(2,1)}) custom-call(f32[8,6,8,128]{3,2,1,0:T(8,128)} %orbitals_ref.1, f32[6,8,128]{2,1,0:T(8,128)} %potential_ref.1), custom_call_target="tpu_custom_call" | custom-call | tf_op jit(solution)/shard_map/gram_exchange/pallas_call | solution.py:320
  58.1 1.3 %constant_dynamic-slice_fusion = f32[8,256]{1,0:T(8,128)} fusion(f32[256,256]{1,0:T(8,128)} %get-tuple-element.4.gram_ref, s32[]{:T(128)S(6)} %select_n.3), kind=kLoop, calls=%fused_computation | loop fusion | bytes 16388 | tf_op jit(solution)/shard_map/dynamic_slice | solution.py:536
  59.4 21.7 %rotation_exchange.1 = f32[8,6,8,128]{3,2,1,0:T(8,128)} custom-call(f32[256,256]{1,0:T(8,128)} %get-tuple-element.4.gram_ref, bf16[256,256]{1,0:T(8,128)(2,1)} %get-tuple-element.5.share_ref), custom_call_target="tpu_custom_call" | custom-call | tf_op jit(solution)/shard_map/rotation_exchange/pallas_call | solution.py:509
  81.1 1.6 %copy.5 = f32[8,6,8,128]{3,2,1,0:T(8,128)} copy(f32[8,6,8,128]{3,2,1,0:T(8,128)} %rotation_exchange.1) | data formatting | bytes 393216

commit v5 on v4

v5 whole, which is shorter than its diff:
```python
import functools

import jax
import jax.numpy as jnp
from jax import lax
from jax.experimental import pallas as pl
from jax.experimental.pallas import tpu as pltpu
from jax.sharding import PartitionSpec as P

stencil_coeffs = (
    -5369.0 / 1800.0,
    12.0 / 7.0,
    -15.0 / 56.0,
    10.0 / 189.0,
    -1.0 / 112.0,
    2.0 / 1925.0,
    -1.0 / 16632.0,
)
spacing = 0.5
low_edge = 5.0
high_edge = 46.0
bottom_edge = -6.5


def filter_scalars():
    half = (high_edge - low_edge) / 2.0
    center = (high_edge + low_edge) / 2.0
    sigma = half / (bottom_edge - center)
    sigma_two = 1.0 / (2.0 / sigma - sigma)
    return (half, center, sigma, sigma_two)


MESH = pl.DeviceIdType.MESH
BANDS = 32
OWNERS = 24
LAYERS = 16
SENDERS = 12
PLANE = 32
GRID_X = 8
GRID_Y = 4
FULL = 256


def owner_band(share):
    return (share // 3) * 4 + share % 3


def band_share(band):
    return (band // 4) * 3 + band % 4


def far_first(step, count):
    reach = (step + 1) // 2
    return count // 2 + reach * (2 * (step % 2) - 1)


def band_partner(band, step):
    side = (band // LAYERS + 1 + step) % 2
    return side * LAYERS + (band % LAYERS + far_first(step // 2, LAYERS)) % LAYERS


def layer_partner(band, step):
    return (band // LAYERS) * LAYERS + (band % LAYERS + far_first(step, LAYERS)) % LAYERS


def plane_partner(place, step):
    across = (place // GRID_Y + far_first(step // GRID_Y, GRID_X)) % GRID_X
    return across * GRID_Y + (place + far_first(step % GRID_Y, GRID_Y)) % GRID_Y


def plane_device(place, layer):
    row = place % GRID_Y
    return {"band": (row // 2) * LAYERS + layer, "gx": place // GRID_Y, "gy": row % 2}


def await_arrivals(buffer, sem):
    pltpu.make_async_copy(buffer, buffer, sem).wait()


def split_parts(value):
    high = value.astype(jnp.bfloat16)
    rest = value - high.astype(jnp.float32)
    middle = rest.astype(jnp.bfloat16)
    return high, middle, (rest - middle.astype(jnp.float32)).astype(jnp.bfloat16)


def inverse_factor(matrix, rows_buf, cols_buf, panel_buf):
    size = matrix.shape[1]
    width = panel_buf.shape[0]
    lane = lax.broadcasted_iota(jnp.int32, (1, size), 1)
    done = []
    for begin in range(0, size, width):
        end = begin + width
        head = matrix[:width]
        rows_buf[...] = head
        for j in range(width):
            cols_buf[j] = jnp.broadcast_to(head[:, begin + j : begin + j + 1], (width, size))
        entry = {}
        for j in range(width):
            for i in range(j, width):
                entry[i, j] = cols_buf[j, i : i + 1, :]
        inside = (lane >= begin) & (lane < end)
        row = [
            jnp.where(inside, (lane == begin + i).astype(jnp.float32), rows_buf[i : i + 1, :])
            for i in range(width)
        ]
        for p in range(width):
            scale = lax.rsqrt(entry[p, p])
            for i in range(p + 1, width):
                entry[i, p] = entry[i, p] * scale
            lead = row[p] * scale
            for i in range(p + 1, width):
                for j in range(p + 1, i + 1):
                    entry[i, j] = entry[i, j] - entry[i, p] * entry[j, p]
                row[i] = row[i] - entry[i, p] * lead
            panel_buf[p : p + 1, :] = lead
        panel = panel_buf[...]
        done.append(jnp.where(jnp.broadcast_to(lane < end, (width, size)), panel, 0.0))
        if end < size:
            high, middle, low = split_parts(panel)
            update = lax.dot_general(
                jnp.concatenate([high, high, middle, high, low, middle], axis=0),
                jnp.concatenate([high, middle, high, low, high, middle], axis=0),
                (((0,), (0,)), ((), ())),
                preferred_element_type=jnp.float32,
            )
            rest = jnp.where(jnp.broadcast_to(inside, (size - end, size)), 0.0, matrix[width:])
            matrix = rest - update[end:]
    return jnp.concatenate(done, axis=0)


def full_dot(left, right, left_dim, right_dim):
    return lax.dot_general(
        left,
        right,
        (((left_dim,), (right_dim,)), ((), ())),
        preferred_element_type=jnp.float32,
        precision=lax.Precision.HIGHEST,
    )


def kinetic(wide, other, at):
    own = wide[6 + at]
    around = other[at]
    column = jnp.concatenate([around, own, around], axis=0)
    total = 3.0 * stencil_coeffs[0] * own
    for m in range(1, 7):
        near = wide[6 + at + m] + wide[6 + at - m]
        near = near + (column[8 + m : 16 + m] + column[8 - m : 16 - m])
        near = near + (pltpu.roll(own, m, 2) + pltpu.roll(own, 128 - m, 2))
        total = total + stencil_coeffs[m] * near
    return own, -0.5 / spacing**2 * total


def filter_rotate_kernel(
    cells,
    orbitals_ref,
    potential_ref,
    rotated_ref,
    gram_ref,
    gram,
    share,
    inverse,
    rows_buf,
    cols_buf,
    panel_buf,
    parcels,
    arrived,
    mine_ref,
    outgoing,
    halos,
    base,
    slope,
    other_side,
    shares,
    partial,
    pieces,
    piece,
    layers,
    total,
    blocks,
    halo_send,
    halo_recv,
    send_sem,
    recv_sem,
    local_sem,
):
    band = lax.axis_index("band")
    layer = band % LAYERS
    place = lax.axis_index("gx") * GRID_Y + (band // LAYERS) * 2 + lax.axis_index("gy")
    owns = band % 4 != 3

    barrier = pltpu.get_barrier_semaphore()

    def greet(device):
        pl.semaphore_signal(barrier, 1, device_id=device, device_id_type=MESH)

    def greet_band(step, carry):
        greet({"band": band_partner(band, step)})
        return carry

    def greet_plane(step, carry):
        other = plane_partner(place, step)
        alike = (other // GRID_Y == lax.axis_index("gx")) & (other % 2 == lax.axis_index("gy"))

        @pl.when(jnp.logical_not(alike))
        def _():
            greet(plane_device(other, layer))

        return carry

    lax.fori_loop(0, BANDS - 1, greet_band, 0)
    lax.fori_loop(0, PLANE - 1, greet_plane, 0)

    def turn(at, carry):
        plane = jnp.swapaxes(orbitals_ref[:, at], 0, 1)
        base[6 + at] = plane
        rows_at = pl.ds(pl.multiple_of(at * 64, 64), 64)
        outgoing[0, rows_at] = plane.reshape(64, 128).astype(jnp.bfloat16)
        return carry

    lax.fori_loop(0, 6, turn, 0)
    pl.semaphore_wait(barrier, BANDS - 1 + PLANE - 2)

    place_x, place_y = lax.axis_index("gx"), lax.axis_index("gy")
    sides = (
        {"gx": (place_x + 1) % 8},
        {"gx": (place_x + 7) % 8},
        {"gy": 1 - place_y},
    )

    def halo_copy(turn_at, side):
        return pltpu.make_async_remote_copy(
            src_ref=outgoing.at[turn_at],
            dst_ref=halos.at[turn_at, side],
            send_sem=halo_send.at[turn_at, side],
            recv_sem=halo_recv.at[turn_at, side],
            device_id=sides[side],
            device_id_type=MESH,
        )

    def halo_take(turn_at, wide):
        for side in range(3):
            halo_copy(turn_at, side).wait_recv()

        def widen(at, carry):
            rows_at = pl.ds(pl.multiple_of(at * 64, 64), 64)
            for side, target, offset in ((0, wide, 0), (1, wide, 12), (2, other_side, 0)):
                block = halos[turn_at, side, rows_at]
                target[at + offset] = block.astype(jnp.float32).reshape(8, 8, 128)
            return carry

        lax.fori_loop(0, 6, widen, 0)

    half, center, sigma, sigma_two = filter_scalars()
    for side in (2, 0, 1):
        halo_copy(0, side).start()
    halo_take(0, base)

    def first_step(at, carry):
        own, moved = kinetic(base, other_side, at)
        shifted = (potential_ref[at] - center)[:, None, :]
        result = sigma / half * (moved + shifted * own)
        slope[6 + at] = result
        rows_at = pl.ds(pl.multiple_of(at * 64, 64), 64)
        outgoing[1, rows_at] = result.reshape(64, 128).astype(jnp.bfloat16)
        return carry

    lax.fori_loop(0, 6, first_step, 0)
    for side in (2, 0, 1):
        halo_copy(1, side).start()
    halo_take(1, slope)

    def second_step(at, carry):
        own, moved = kinetic(slope, other_side, at)
        shifted = (potential_ref[at] - center)[:, None, :]
        result = 2.0 * sigma_two / half * (moved + shifted * own) - sigma * sigma_two * base[6 + at]
        rows_at = pl.ds(pl.multiple_of(at * 64, 64), 64)
        mine_ref[rows_at] = result.reshape(64, 128).astype(jnp.bfloat16)
        return carry

    lax.fori_loop(0, 6, second_step, 0)

    def remote(source, target, phase, device):
        return pltpu.make_async_remote_copy(
            src_ref=source,
            dst_ref=target,
            send_sem=send_sem.at[phase],
            recv_sem=recv_sem.at[phase],
            device_id=device,
            device_id_type=MESH,
        )

    def cell_share(step, carry):
        other = band_partner(band, step)

        @pl.when(other % 4 != 3)
        def _():
            at = pl.multiple_of(band_share(other) * 16, 16)
            to = pl.multiple_of(band * 16, 16)
            remote(
                mine_ref.at[pl.ds(at, 16)], shares.at[pl.ds(to, 16)], 0, {"band": other}
            ).start()

        return carry

    lax.fori_loop(0, BANDS - 1, cell_share, 0)

    @pl.when(owns)
    def _():
        at = pl.multiple_of(band_share(band) * 16, 16)
        to = pl.multiple_of(band * 16, 16)
        own = pltpu.make_async_copy(
            mine_ref.at[pl.ds(at, 16)], shares.at[pl.ds(to, 16)], local_sem
        )
        own.start()
        own.wait()
        await_arrivals(shares.at[pl.ds(0, 16 * (BANDS - 1))], recv_sem.at[0])
        spread = shares[...].astype(jnp.float32).reshape(BANDS, 2, 8, 128)
        halves = [spread[:, half].reshape(FULL, 128) for half in range(2)]
        both = jnp.concatenate(halves, axis=1).astype(jnp.bfloat16)
        share[...] = both
        local = lax.dot_general(
            both, both, (((1,), (1,)), ((), ())), preferred_element_type=jnp.float32
        )
        sides = [local[:, 128 * h : 128 * h + 128].reshape(PLANE, 1, 8, 128) for h in range(2)]
        partial[...] = (
            jnp.concatenate(sides, axis=1).reshape(PLANE, 16, 128).astype(jnp.bfloat16)
        )

        def send_piece(step, carry):
            other = plane_partner(place, step)
            remote(
                partial.at[other], pieces.at[place], 1, plane_device(other, layer)
            ).start()
            return carry

        lax.fori_loop(0, PLANE - 1, send_piece, 0)
        pieces[place] = partial[place]
        await_arrivals(pieces.at[pl.ds(0, PLANE - 1)], recv_sem.at[1])
        piece[...] = jnp.sum(pieces[...].astype(jnp.float32), axis=0).astype(jnp.bfloat16)
        at_layer = band_share(layer)

        def send_layer(step, carry):
            remote(
                piece, layers.at[at_layer], 2, {"band": layer_partner(band, step)}
            ).start()
            return carry

        lax.fori_loop(0, LAYERS - 1, send_layer, 0)
        layers[at_layer] = piece[...]
        await_arrivals(layers.at[pl.ds(0, SENDERS - 1)], recv_sem.at[2])

    @pl.when(jnp.logical_not(owns))
    def _():
        await_arrivals(layers, recv_sem.at[2])

    total[...] = jnp.sum(layers[...].astype(jnp.float32), axis=0) / cells

    def send_total(step, carry):
        other = plane_partner(place, step)
        remote(total, blocks.at[place], 3, plane_device(other, layer)).start()
        return carry

    lax.fori_loop(0, PLANE - 1, send_total, 0)
    blocks[place] = total[...]
    await_arrivals(blocks.at[pl.ds(0, PLANE - 1)], recv_sem.at[3])
    found = blocks[...]
    gram[:, :128] = found[:, :8].reshape(FULL, 128)
    gram[:, 128:] = found[:, 8:].reshape(FULL, 128)
    gram_ref[...] = gram[pl.ds(pl.multiple_of(band * 8, 8), 8), :]

    @pl.when(owns)
    def _():
        to = pl.multiple_of(band_share(band) * 16, 16)

        def send_parcels(side, weights, cells_of):
            turned = jnp.dot(weights, cells_of, preferred_element_type=jnp.float32)
            halves = [
                turned[:, 128 * h : 128 * h + 128].reshape(LAYERS, 1, 8, 128) for h in range(2)
            ]
            base_row = side * LAYERS * 16
            parcels[base_row : base_row + LAYERS * 16] = (
                jnp.concatenate(halves, axis=1).reshape(LAYERS * 16, 128).astype(jnp.bfloat16)
            )

            def send_parcel(step, carry):
                other = side * LAYERS + (layer + far_first(step, LAYERS)) % LAYERS
                at = pl.multiple_of(other * 16, 16)

                @pl.when(other != band)
                def _():
                    remote(
                        parcels.at[pl.ds(at, 16)], arrived.at[pl.ds(to, 16)], 4, {"band": other}
                    ).start()

                return carry

            lax.fori_loop(0, LAYERS, send_parcel, 0)

        buffers = (rows_buf, cols_buf, panel_buf)
        upper = inverse_factor(gram[:128, :128], *buffers)
        send_parcels(0, upper.astype(jnp.bfloat16), share[:128])
        lower_left = full_dot(gram[128:, :128], upper, 1, 1)
        remaining = gram[128:, 128:] - full_dot(lower_left, lower_left, 1, 1)
        carried = full_dot(lower_left, upper, 1, 0)
        lower = inverse_factor(remaining, *buffers)
        inverse[:, 128:] = lower.astype(jnp.bfloat16)
        inverse[:, :128] = (-full_dot(lower, carried, 1, 0)).astype(jnp.bfloat16)
        send_parcels(1, inverse[...], share[...])
        at = pl.multiple_of(band * 16, 16)
        own = pltpu.make_async_copy(
            parcels.at[pl.ds(at, 16)], arrived.at[pl.ds(to, 16)], local_sem
        )
        own.start()
        own.wait()
        await_arrivals(arrived.at[pl.ds(0, 16 * (OWNERS - 1))], recv_sem.at[4])

    @pl.when(jnp.logical_not(owns))
    def _():
        await_arrivals(arrived, recv_sem.at[4])

    rotated_ref[...] = arrived[...]

    @pl.when(owns)
    def _():
        await_arrivals(parcels.at[pl.ds(0, 16 * (BANDS - 1))], send_sem.at[4])
        await_arrivals(mine_ref.at[pl.ds(0, 16 * (OWNERS - 1))], send_sem.at[0])
        await_arrivals(pieces.at[pl.ds(0, PLANE - 1)], send_sem.at[1])
        await_arrivals(pieces.at[pl.ds(0, LAYERS - 1)], send_sem.at[2])

    @pl.when(jnp.logical_not(owns))
    def _():
        await_arrivals(mine_ref, send_sem.at[0])

    for turn_at in range(2):
        for side in range(3):
            halo_copy(turn_at, side).wait_send()
    await_arrivals(blocks.at[pl.ds(0, PLANE - 1)], send_sem.at[3])


def filter_rotate(orbitals, potential, cells):
    return pl.pallas_call(
        functools.partial(filter_rotate_kernel, cells),
        out_shape=(
            jax.ShapeDtypeStruct((OWNERS * 16, 128), jnp.bfloat16),
            jax.ShapeDtypeStruct((8, FULL), jnp.float32),
        ),
        in_specs=[pl.BlockSpec(memory_space=pltpu.VMEM)] * 2,
        out_specs=(pl.BlockSpec(memory_space=pltpu.VMEM),) * 2,
        scratch_shapes=[
            pltpu.VMEM((FULL, FULL), jnp.float32),
            pltpu.VMEM((FULL, FULL), jnp.bfloat16),
            pltpu.VMEM((128, FULL), jnp.bfloat16),
            pltpu.VMEM((16, 128), jnp.float32),
            pltpu.VMEM((16, 16, 128), jnp.float32),
            pltpu.VMEM((16, 128), jnp.float32),
            pltpu.VMEM((BANDS * 16, 128), jnp.bfloat16),
            pltpu.VMEM((OWNERS * 16, 128), jnp.bfloat16),
            pltpu.VMEM((384, 128), jnp.bfloat16),
            pltpu.VMEM((2, 384, 128), jnp.bfloat16),
            pltpu.VMEM((2, 3, 384, 128), jnp.bfloat16),
            pltpu.VMEM((18, 8, 8, 128), jnp.float32),
            pltpu.VMEM((18, 8, 8, 128), jnp.float32),
            pltpu.VMEM((6, 8, 8, 128), jnp.float32),
            pltpu.VMEM((BANDS * 16, 128), jnp.bfloat16),
            pltpu.VMEM((PLANE, 16, 128), jnp.bfloat16),
            pltpu.VMEM((PLANE, 16, 128), jnp.bfloat16),
            pltpu.VMEM((16, 128), jnp.bfloat16),
            pltpu.VMEM((SENDERS, 16, 128), jnp.bfloat16),
            pltpu.VMEM((16, 128), jnp.float32),
            pltpu.VMEM((PLANE, 16, 128), jnp.float32),
            pltpu.SemaphoreType.DMA((2, 3)),
            pltpu.SemaphoreType.DMA((2, 3)),
            pltpu.SemaphoreType.DMA((5,)),
            pltpu.SemaphoreType.DMA((5,)),
            pltpu.SemaphoreType.DMA,
        ],
        compiler_params=pltpu.CompilerParams(collective_id=1, has_side_effects=True),
        name="filter_rotate",
    )(orbitals, potential)


def body(orbitals, potential):
    count, size_x, size_y, size_z = orbitals.shape
    total_cells = size_x * size_y * size_z * lax.axis_size("gx") * lax.axis_size("gy")
    tiles, gram_rows = filter_rotate(orbitals, potential, float(total_cells))
    rotated = tiles.astype(jnp.float32).reshape(size_x, size_y, count, size_z).transpose(2, 0, 1, 3)
    return (rotated, gram_rows)


def solution(mesh):
    return jax.shard_map(
        body,
        mesh=mesh,
        in_specs=(P("band", "gx", "gy", None), P("gx", "gy", None)),
        out_specs=(P("band", "gx", "gy", None), P("band", None)),
        check_vma=False,
    )
```

time: 82.9 us -> 76.8 us (0.926)
  the two profiles are of different devices: /device:TPU:2 before, /device:TPU:24 now
where the time goes in v5:
time: 76.8 us; the launch traced here: 76.7 us
  Pallas kernels  73.8 us (96%)
  local copies, waits for them, and re-layouts  2.19 us (3%)
    pallas_call x1, Pallas kernels, filter_rotate(): pl.pallas_call(functools.partial(filter_rotate_kernel, cells), out_shape=...  73.8 us
    transpose x1, local copies, waits for them, and re-layouts, body(): tiles.astype(jnp.float32).reshape(size_x, size_y, count, size_z)  1.59 us

profile of v5, /device:TPU:24, one launch (start us, length us, event | category | flops | bytes accessed | tf_op | source)
XLA Modules:
  0.0 76.7 jit_solution(11129753386724633350)
XLA Ops:
  0.6 73.8 %filter_rotate.1 = (bf16[384,128]{1,0:T(8,128)(2,1)}, f32[8,256]{1,0:T(8,128)}) custom-call(f32[8,6,8,128]{3,2,1,0:T(8,128)} %orbitals_ref.1, f32[6,8,128]{2,1,0:T(8,128)} %potential_ref.1), custom_call_target="tpu_custom_call" | custom-call | tf_op jit(solution)/shard_map/filter_rotate/pallas_call | solution.py:443
  74.5 0.0 copy-start
  74.5 1.6 %copy.6 = f32[6,8,8,128]{3,1,0,2:T(8,128)} copy(bf16[6,8,8,128]{3,2,1,0:T(8,128)(2,1)} %bitcast.6) | data formatting | bytes 294912 | tf_op jit(solution)/shard_map/transpose | solution.py:488
  76.1 0.0 copy-done
  76.1 0.6 copy.8
Async XLA Ops:
  74.5 1.6 %copy-start = (f32[8,256]{1,0:T(8,128)S(1)}, f32[8,256]{1,0:T(8,128)}, u32[]{:S(2)}) copy-start(f32[8,256]{1,0:T(8,128)} %get-tuple-element.9) | copy-start | bytes 24580

commit v6 on v5

--- a/solution.py
+++ b/solution.py
@@ -54,23 +54,13 @@
     return count // 2 + reach * (2 * (step % 2) - 1)
 
 
-def band_partner(band, step):
-    side = (band // LAYERS + 1 + step) % 2
-    return side * LAYERS + (band % LAYERS + far_first(step // 2, LAYERS)) % LAYERS
-
-
-def layer_partner(band, step):
-    return (band // LAYERS) * LAYERS + (band % LAYERS + far_first(step, LAYERS)) % LAYERS
+def spot(across, row, layer):
+    return {"band": (row // 2) * LAYERS + layer, "gx": across, "gy": row % 2}
 
 
 def plane_partner(place, step):
     across = (place // GRID_Y + far_first(step // GRID_Y, GRID_X)) % GRID_X
     return across * GRID_Y + (place + far_first(step % GRID_Y, GRID_Y)) % GRID_Y
-
-
-def plane_device(place, layer):
-    row = place % GRID_Y
-    return {"band": (row // 2) * LAYERS + layer, "gx": place // GRID_Y, "gy": row % 2}
 
 
 def await_arrivals(buffer, sem):
@@ -183,34 +173,31 @@
     halo_recv,
     send_sem,
     recv_sem,
-    local_sem,
+    tokens,
 ):
     band = lax.axis_index("band")
     layer = band % LAYERS
-    place = lax.axis_index("gx") * GRID_Y + (band // LAYERS) * 2 + lax.axis_index("gy")
+    across = lax.axis_index("gx")
+    half_y = lax.axis_index("gy")
+    row = (band // LAYERS) * 2 + half_y
+    place = across * GRID_Y + row
     owns = band % 4 != 3
 
+    def near(step_x, step_y, step_z):
+        return spot(
+            (across + step_x) % GRID_X, (row + step_y) % GRID_Y, (layer + step_z) % LAYERS
+        )
+
     barrier = pltpu.get_barrier_semaphore()
-
-    def greet(device):
+    greeted = [near(0, 0, step) for step in (3, -3, 2, -2, 1, -1)]
+    greeted += [near(0, side, step) for step in (2, -2, 1, -1, 0) for side in (1, 3)]
+    greeted += [near(1, 0, 0), near(-1, 0, 0)]
+    for device in greeted:
         pl.semaphore_signal(barrier, 1, device_id=device, device_id_type=MESH)
 
-    def greet_band(step, carry):
-        greet({"band": band_partner(band, step)})
-        return carry
-
-    def greet_plane(step, carry):
-        other = plane_partner(place, step)
-        alike = (other // GRID_Y == lax.axis_index("gx")) & (other % 2 == lax.axis_index("gy"))
-
-        @pl.when(jnp.logical_not(alike))
-        def _():
-            greet(plane_device(other, layer))
-
-        return carry
-
-    lax.fori_loop(0, BANDS - 1, greet_band, 0)
-    lax.fori_loop(0, PLANE - 1, greet_plane, 0)
+    def send_tokens(kind, devices):
+        for device in devices:
+            pl.semaphore_signal(tokens.at[kind], 1, device_id=device, device_id_type=MESH)
 
     def turn(at, carry):
         plane = jnp.swapaxes(orbitals_ref[:, at], 0, 1)
@@ -220,14 +207,10 @@
         return carry
 
     lax.fori_loop(0, 6, turn, 0)
-    pl.semaphore_wait(barrier, BANDS - 1 + PLANE - 2)
-
-    place_x, place_y = lax.axis_index("gx"), lax.axis_index("gy")
-    sides = (
-        {"gx": (place_x + 1) % 8},
-        {"gx": (place_x + 7) % 8},
-        {"gy": 1 - place_y},
-    )
+    pl.semaphore_wait(barrier, len(greeted))
+    send_tokens(0, (near(0, 0, 3), near(0, 0, -3)))
+
+    sides = (near(1, 0, 0), near(-1, 0, 0), {"gy": 1 - half_y})
 
     def halo_copy(turn_at, side):
         return pltpu.make_async_remote_copy(
@@ -256,6 +239,8 @@
     for side in (2, 0, 1):
         halo_copy(0, side).start()
     halo_take(0, base)
+    pl.semaphore_wait(tokens.at[0], 2)
+    send_tokens(1, (near(0, 0, 5), near(0, 0, -5)))
 
     def first_step(at, carry):
         own, moved = kinetic(base, other_side, at)
@@ -270,6 +255,7 @@
     for side in (2, 0, 1):
         halo_copy(1, side).start()
     halo_take(1, slope)
+    send_tokens(2, (near(3, 0, 0), near(-3, 0, 0)))
 
     def second_step(at, carry):
         own, moved = kinetic(slope, other_side, at)
@@ -292,30 +278,30 @@
         )
 
     def cell_share(step, carry):
-        other = band_partner(band, step)
+        to_row = (row + 1 + 2 * (step % 2)) % GRID_Y
+        to_layer = (layer + far_first(step // 2, LAYERS)) % LAYERS
+        other = (to_row // 2) * LAYERS + to_layer
 
         @pl.when(other % 4 != 3)
         def _():
             at = pl.multiple_of(band_share(other) * 16, 16)
             to = pl.multiple_of(band * 16, 16)
             remote(
-                mine_ref.at[pl.ds(at, 16)], shares.at[pl.ds(to, 16)], 0, {"band": other}
+                mine_ref.at[pl.ds(at, 16)],
+                shares.at[pl.ds(to, 16)],
+                0,
+                {"band": other, "gy": 1 - half_y},
             ).start()
 
         return carry
 
-    lax.fori_loop(0, BANDS - 1, cell_share, 0)
+    pl.semaphore_wait(tokens.at[1], 2)
+    lax.fori_loop(0, BANDS, cell_share, 0)
+    pl.semaphore_wait(tokens.at[2], 2)
 
     @pl.when(owns)
     def _():
-        at = pl.multiple_of(band_share(band) * 16, 16)
-        to = pl.multiple_of(band * 16, 16)
-        own = pltpu.make_async_copy(
-            mine_ref.at[pl.ds(at, 16)], shares.at[pl.ds(to, 16)], local_sem
-        )
-        own.start()
-        own.wait()
-        await_arrivals(shares.at[pl.ds(0, 16 * (BANDS - 1))], recv_sem.at[0])
+        await_arrivals(shares, recv_sem.at[0])
         spread = shares[...].astype(jnp.float32).reshape(BANDS, 2, 8, 128)
         halves = [spread[:, half].reshape(FULL, 128) for half in range(2)]
         both = jnp.concatenate(halves, axis=1).astype(jnp.bfloat16)
@@ -331,7 +317,10 @@
         def send_piece(step, carry):
             other = plane_partner(place, step)
             remote(
-                partial.at[other], pieces.at[place], 1, plane_device(other, layer)
+                partial.at[other],
+                pieces.at[place],
+                1,
+                spot(other // GRID_Y, other % GRID_Y, layer),
             ).start()
             return carry
 
@@ -343,7 +332,10 @@
 
         def send_layer(step, carry):
             remote(
-                piece, layers.at[at_layer], 2, {"band": layer_partner(band, step)}
+                piece,
+                layers.at[at_layer],
+                2,
+                spot(across, row, (layer + far_first(step, LAYERS)) % LAYERS),
             ).start()
             return carry
 
@@ -359,7 +351,9 @@
 
     def send_total(step, carry):
         other = plane_partner(place, step)
-        remote(total, blocks.at[place], 3, plane_device(other, layer)).start()
+        remote(
+            total, blocks.at[place], 3, spot(other // GRID_Y, other % GRID_Y, layer)
+        ).start()
         return carry
 
     lax.fori_loop(0, PLANE - 1, send_total, 0)
@@ -387,13 +381,12 @@
             def send_parcel(step, carry):
                 other = side * LAYERS + (layer + far_first(step, LAYERS)) % LAYERS
                 at = pl.multiple_of(other * 16, 16)
-
-                @pl.when(other != band)
-                def _():
-                    remote(
-                        parcels.at[pl.ds(at, 16)], arrived.at[pl.ds(to, 16)], 4, {"band": other}
-                    ).start()
-
+                remote(
+                    parcels.at[pl.ds(at, 16)],
+                    arrived.at[pl.ds(to, 16)],
+                    4,
+                    {"band": other, "gy": 1 - half_y},
+                ).start()
                 return carry
 
             lax.fori_loop(0, LAYERS, send_parcel, 0)
@@ -408,31 +401,17 @@
         inverse[:, 128:] = lower.astype(jnp.bfloat16)
         inverse[:, :128] = (-full_dot(lower, carried, 1, 0)).astype(jnp.bfloat16)
         send_parcels(1, inverse[...], share[...])
-        at = pl.multiple_of(band * 16, 16)
-        own = pltpu.make_async_copy(
-            parcels.at[pl.ds(at, 16)], arrived.at[pl.ds(to, 16)], local_sem
-        )
-        own.start()
-        own.wait()
-        await_arrivals(arrived.at[pl.ds(0, 16 * (OWNERS - 1))], recv_sem.at[4])
-
-    @pl.when(jnp.logical_not(owns))
-    def _():
-        await_arrivals(arrived, recv_sem.at[4])
-
+
+    await_arrivals(arrived, recv_sem.at[4])
     rotated_ref[...] = arrived[...]
 
     @pl.when(owns)
     def _():
-        await_arrivals(parcels.at[pl.ds(0, 16 * (BANDS - 1))], send_sem.at[4])
-        await_arrivals(mine_ref.at[pl.ds(0, 16 * (OWNERS - 1))], send_sem.at[0])
+        await_arrivals(parcels, send_sem.at[4])
         await_arrivals(pieces.at[pl.ds(0, PLANE - 1)], send_sem.at[1])
         await_arrivals(pieces.at[pl.ds(0, LAYERS - 1)], send_sem.at[2])
 
-    @pl.when(jnp.logical_not(owns))
-    def _():
-        await_arrivals(mine_ref, send_sem.at[0])
-
+    await_arrivals(mine_ref, send_sem.at[0])
     for turn_at in range(2):
         for side in range(3):
             halo_copy(turn_at, side).wait_send()
@@ -474,7 +453,7 @@
             pltpu.SemaphoreType.DMA((2, 3)),
             pltpu.SemaphoreType.DMA((5,)),
             pltpu.SemaphoreType.DMA((5,)),
-            pltpu.SemaphoreType.DMA,
+            pltpu.SemaphoreType.REGULAR((3,)),
         ],
         compiler_params=pltpu.CompilerParams(collective_id=1, has_side_effects=True),
         name="filter_rotate",

time: 76.8 us -> 73.3 us (0.954)
  Pallas kernels: 73.8 us -> 70.3 us
    pallas_call x1, Pallas kernels: 73.8 us -> 70.3 us  [filter_rotate(): pl.pallas_call(functools.partial(filter_rotate_kernel, cells), out_shape=...]
where the time goes in v6:
time: 73.3 us; the launch traced here: 73.2 us
  Pallas kernels  70.3 us (96%)
  local copies, waits for them, and re-layouts  2.19 us (3%)
    pallas_call x1, Pallas kernels, filter_rotate(): pl.pallas_call(functools.partial(filter_rotate_kernel, cells), out_shape=...  70.3 us
    transpose x1, local copies, waits for them, and re-layouts, body(): tiles.astype(jnp.float32).reshape(size_x, size_y, count, size_z)  1.59 us

profile of v6, /device:TPU:24, one launch (start us, length us, event | category | flops | bytes accessed | tf_op | source)
XLA Modules:
  0.0 73.2 jit_solution(958286402164985005)
XLA Ops:
  0.6 70.3 %filter_rotate.1 = (bf16[384,128]{1,0:T(8,128)(2,1)}, f32[8,256]{1,0:T(8,128)}) custom-call(f32[8,6,8,128]{3,2,1,0:T(8,128)} %orbitals_ref.1, f32[6,8,128]{2,1,0:T(8,128)} %potential_ref.1), custom_call_target="tpu_custom_call" | custom-call | tf_op jit(solution)/shard_map/filter_rotate/pallas_call | solution.py:422
  71.0 0.0 copy-start
  71.0 1.6 %copy.6 = f32[6,8,8,128]{3,1,0,2:T(8,128)} copy(bf16[6,8,8,128]{3,2,1,0:T(8,128)(2,1)} %bitcast.6) | data formatting | bytes 294912 | tf_op jit(solution)/shard_map/transpose | solution.py:467
  72.6 0.0 copy-done
  72.6 0.6 copy.8
Async XLA Ops:
  71.0 1.6 %copy-start = (f32[8,256]{1,0:T(8,128)S(1)}, f32[8,256]{1,0:T(8,128)}, u32[]{:S(2)}) copy-start(f32[8,256]{1,0:T(8,128)} %get-tuple-element.9) | copy-start | bytes 24580

commit v7 on v6

--- a/solution.py
+++ b/solution.py
@@ -36,6 +36,7 @@
 LAYERS = 16
 SENDERS = 12
 PLANE = 32
+HOLDERS = 24
 GRID_X = 8
 GRID_Y = 4
 FULL = 256
@@ -75,57 +76,83 @@
 
 
 def inverse_factor(matrix, rows_buf, cols_buf, panel_buf):
-    size = matrix.shape[1]
-    width = panel_buf.shape[0]
-    lane = lax.broadcasted_iota(jnp.int32, (1, size), 1)
+    tile, size = 8, 128
+    count = size // tile
+    lane = lax.broadcasted_iota(jnp.int32, (tile, size), 1)
+
+    def full(value):
+        return jnp.broadcast_to(value, (tile, size))
+
+    tiles = [matrix[tile * t : tile * t + tile] for t in range(count)]
     done = []
-    for begin in range(0, size, width):
-        end = begin + width
-        head = matrix[:width]
-        rows_buf[...] = head
-        for j in range(width):
-            cols_buf[j] = jnp.broadcast_to(head[:, begin + j : begin + j + 1], (width, size))
-        entry = {}
-        for j in range(width):
-            for i in range(j, width):
-                entry[i, j] = cols_buf[j, i : i + 1, :]
-        inside = (lane >= begin) & (lane < end)
+    for now in range(count):
+        begin, slot = tile * now, now % 2
+        head = tiles[now]
+        rows_buf[slot] = head
+        for j in range(tile):
+            cols_buf[slot, j] = full(head[:, begin + j : begin + j + 1])
+        inside = (lane >= begin) & (lane < begin + tile)
+        entry = {
+            (i, j): full(cols_buf[slot, j, i : i + 1, :])
+            for j in range(tile)
+            for i in range(j, tile)
+        }
         row = [
-            jnp.where(inside, (lane == begin + i).astype(jnp.float32), rows_buf[i : i + 1, :])
-            for i in range(width)
+            jnp.where(
+                inside,
+                (lane == begin + i).astype(jnp.float32),
+                full(rows_buf[slot, i : i + 1, :]),
+            )
+            for i in range(tile)
         ]
-        for p in range(width):
+        follows = now + 1 < count
+        if follows:
+            after = tiles[now + 1]
+            column = [full(after[:, begin + p : begin + p + 1]) for p in range(tile)]
+            after = jnp.where(inside, 0.0, after)
+        scales = []
+        for p in range(tile):
             scale = lax.rsqrt(entry[p, p])
-            for i in range(p + 1, width):
+            scales.append(scale)
+            for i in range(p + 1, tile):
                 entry[i, p] = entry[i, p] * scale
-            lead = row[p] * scale
-            for i in range(p + 1, width):
+            row[p] = row[p] * scale
+            if follows:
+                column[p] = column[p] * scale
+                after = after - column[p] * row[p]
+            for i in range(p + 1, tile):
                 for j in range(p + 1, i + 1):
                     entry[i, j] = entry[i, j] - entry[i, p] * entry[j, p]
-                row[i] = row[i] - entry[i, p] * lead
-            panel_buf[p : p + 1, :] = lead
-        panel = panel_buf[...]
-        done.append(jnp.where(jnp.broadcast_to(lane < end, (width, size)), panel, 0.0))
-        if end < size:
-            high, middle, low = split_parts(panel)
-            update = lax.dot_general(
-                jnp.concatenate([high, high, middle, high, low, middle], axis=0),
-                jnp.concatenate([high, middle, high, low, high, middle], axis=0),
-                (((0,), (0,)), ((), ())),
-                preferred_element_type=jnp.float32,
-            )
-            rest = jnp.where(jnp.broadcast_to(inside, (size - end, size)), 0.0, matrix[width:])
-            matrix = rest - update[end:]
+                row[i] = row[i] - entry[i, p] * row[p]
+                if follows:
+                    column[i] = column[i] - column[p] * entry[i, p]
+            panel_buf[slot, p : p + 1, :] = row[p][:1]
+        if follows:
+            tiles[now + 1] = after
+        done.append(jnp.where(lane < begin + tile, panel_buf[slot], 0.0))
+        if now + 2 < count:
+            solved = [None] * tile
+            for p in range(tile - 1, -1, -1):
+                value = row[p]
+                for i in range(p + 1, tile):
+                    value = value - entry[i, p] * solved[i]
+                solved[p] = value * scales[p]
+            for t in range(now + 2, count):
+                value = jnp.where(inside, 0.0, tiles[t])
+                for p in range(tile):
+                    value = value - full(tiles[t][:, begin + p : begin + p + 1]) * solved[p]
+                tiles[t] = value
     return jnp.concatenate(done, axis=0)
 
 
 def full_dot(left, right, left_dim, right_dim):
+    a, b, c = split_parts(left)
+    d, e, f = split_parts(right)
     return lax.dot_general(
-        left,
-        right,
+        jnp.concatenate([a, a, b, a, c, b], axis=left_dim),
+        jnp.concatenate([d, e, d, f, d, e], axis=right_dim),
         (((left_dim,), (right_dim,)), ((), ())),
         preferred_element_type=jnp.float32,
-        precision=lax.Precision.HIGHEST,
     )
 
 
@@ -183,6 +210,15 @@
     place = across * GRID_Y + row
     owns = band % 4 != 3
 
+    def holds_piece(spot_x, spot_y):
+        return (spot_x + spot_y) % 4 != 3
+
+    def piece_of(spot_x, spot_y):
+        return spot_x * 3 + (spot_x + spot_y) % 4
+
+    holds = holds_piece(across, row)
+    own_piece = piece_of(across, row)
+
     def near(step_x, step_y, step_z):
         return spot(
             (across + step_x) % GRID_X, (row + step_y) % GRID_Y, (layer + step_z) % LAYERS
@@ -306,26 +342,35 @@
         halves = [spread[:, half].reshape(FULL, 128) for half in range(2)]
         both = jnp.concatenate(halves, axis=1).astype(jnp.bfloat16)
         share[...] = both
-        local = lax.dot_general(
-            both, both, (((1,), (1,)), ((), ())), preferred_element_type=jnp.float32
+        first = lax.dot_general(
+            both[:128], both[:128], (((1,), (1,)), ((), ())), preferred_element_type=jnp.float32
         )
-        sides = [local[:, 128 * h : 128 * h + 128].reshape(PLANE, 1, 8, 128) for h in range(2)]
-        partial[...] = (
-            jnp.concatenate(sides, axis=1).reshape(PLANE, 16, 128).astype(jnp.bfloat16)
+        second = lax.dot_general(
+            both[128:], both, (((1,), (1,)), ((), ())), preferred_element_type=jnp.float32
         )
+        blocked = jnp.concatenate([first, second[:, :128], second[:, 128:]], axis=0)
+        partial[...] = blocked.astype(jnp.bfloat16).reshape(HOLDERS, 16, 128)
 
         def send_piece(step, carry):
             other = plane_partner(place, step)
-            remote(
-                partial.at[other],
-                pieces.at[place],
-                1,
-                spot(other // GRID_Y, other % GRID_Y, layer),
-            ).start()
+            other_x, other_y = other // GRID_Y, other % GRID_Y
+
+            @pl.when(holds_piece(other_x, other_y))
+            def _():
+                remote(
+                    partial.at[piece_of(other_x, other_y)],
+                    pieces.at[place],
+                    1,
+                    spot(other_x, other_y, layer),
+                ).start()
+
             return carry
 
         lax.fori_loop(0, PLANE - 1, send_piece, 0)
-        pieces[place] = partial[place]
+
+    @pl.when(owns & holds)
+    def _():
+        pieces[place] = partial[own_piece]
         await_arrivals(pieces.at[pl.ds(0, PLANE - 1)], recv_sem.at[1])
         piece[...] = jnp.sum(pieces[...].astype(jnp.float32), axis=0).astype(jnp.bfloat16)
         at_layer = band_share(layer)
@@ -343,26 +388,28 @@
         layers[at_layer] = piece[...]
         await_arrivals(layers.at[pl.ds(0, SENDERS - 1)], recv_sem.at[2])
 
-    @pl.when(jnp.logical_not(owns))
+    @pl.when(jnp.logical_not(owns) & holds)
     def _():
         await_arrivals(layers, recv_sem.at[2])
 
-    total[...] = jnp.sum(layers[...].astype(jnp.float32), axis=0) / cells
-
-    def send_total(step, carry):
-        other = plane_partner(place, step)
-        remote(
-            total, blocks.at[place], 3, spot(other // GRID_Y, other % GRID_Y, layer)
-        ).start()
-        return carry
-
-    lax.fori_loop(0, PLANE - 1, send_total, 0)
-    blocks[place] = total[...]
-    await_arrivals(blocks.at[pl.ds(0, PLANE - 1)], recv_sem.at[3])
-    found = blocks[...]
-    gram[:, :128] = found[:, :8].reshape(FULL, 128)
-    gram[:, 128:] = found[:, 8:].reshape(FULL, 128)
-    gram_ref[...] = gram[pl.ds(pl.multiple_of(band * 8, 8), 8), :]
+    @pl.when(holds)
+    def _():
+        total[...] = jnp.sum(layers[...].astype(jnp.float32), axis=0) / cells
+
+        def send_total(step, carry):
+            other = plane_partner(place, step)
+            remote(
+                total, blocks.at[own_piece], 3, spot(other // GRID_Y, other % GRID_Y, layer)
+            ).start()
+            return carry
+
+        lax.fori_loop(0, PLANE - 1, send_total, 0)
+        blocks[own_piece] = total[...]
+        await_arrivals(blocks.at[pl.ds(0, HOLDERS - 1)], recv_sem.at[3])
+
+    @pl.when(jnp.logical_not(holds))
+    def _():
+        await_arrivals(blocks.at[pl.ds(0, HOLDERS)], recv_sem.at[3])
 
     @pl.when(owns)
     def _():
@@ -392,30 +439,48 @@
             lax.fori_loop(0, LAYERS, send_parcel, 0)
 
         buffers = (rows_buf, cols_buf, panel_buf)
-        upper = inverse_factor(gram[:128, :128], *buffers)
+        corner = blocks[8:16].reshape(128, 128)
+        upper = inverse_factor(blocks[0:8].reshape(128, 128), *buffers)
         send_parcels(0, upper.astype(jnp.bfloat16), share[:128])
-        lower_left = full_dot(gram[128:, :128], upper, 1, 1)
-        remaining = gram[128:, 128:] - full_dot(lower_left, lower_left, 1, 1)
+        lower_left = full_dot(corner, upper, 1, 1)
+        remaining = blocks[16:24].reshape(128, 128) - full_dot(lower_left, lower_left, 1, 1)
         carried = full_dot(lower_left, upper, 1, 0)
         lower = inverse_factor(remaining, *buffers)
         inverse[:, 128:] = lower.astype(jnp.bfloat16)
         inverse[:, :128] = (-full_dot(lower, carried, 1, 0)).astype(jnp.bfloat16)
         send_parcels(1, inverse[...], share[...])
 
+    middle_block = blocks[8:16].reshape(128, 128)
+    gram[:128, :128] = blocks[0:8].reshape(128, 128)
+    gram[:128, 128:] = middle_block.T
+    gram[128:, :128] = middle_block
+    gram[128:, 128:] = blocks[16:24].reshape(128, 128)
+    gram_ref[...] = gram[pl.ds(pl.multiple_of(band * 8, 8), 8), :]
+
     await_arrivals(arrived, recv_sem.at[4])
     rotated_ref[...] = arrived[...]
 
     @pl.when(owns)
     def _():
         await_arrivals(parcels, send_sem.at[4])
-        await_arrivals(pieces.at[pl.ds(0, PLANE - 1)], send_sem.at[1])
+
+    @pl.when(owns & holds)
+    def _():
+        await_arrivals(partial.at[pl.ds(0, HOLDERS - 1)], send_sem.at[1])
         await_arrivals(pieces.at[pl.ds(0, LAYERS - 1)], send_sem.at[2])
+
+    @pl.when(owns & jnp.logical_not(holds))
+    def _():
+        await_arrivals(partial, send_sem.at[1])
 
     await_arrivals(mine_ref, send_sem.at[0])
     for turn_at in range(2):
         for side in range(3):
             halo_copy(turn_at, side).wait_send()
-    await_arrivals(blocks.at[pl.ds(0, PLANE - 1)], send_sem.at[3])
+
+    @pl.when(holds)
+    def _():
+        await_arrivals(blocks.at[pl.ds(0, PLANE - 1)], send_sem.at[3])
 
 
 def filter_rotate(orbitals, potential, cells):
@@ -431,9 +496,9 @@
             pltpu.VMEM((FULL, FULL), jnp.float32),
             pltpu.VMEM((FULL, FULL), jnp.bfloat16),
             pltpu.VMEM((128, FULL), jnp.bfloat16),
-            pltpu.VMEM((16, 128), jnp.float32),
-            pltpu.VMEM((16, 16, 128), jnp.float32),
-            pltpu.VMEM((16, 128), jnp.float32),
+            pltpu.VMEM((2, 8, 128), jnp.float32),
+            pltpu.VMEM((2, 8, 8, 128), jnp.float32),
+            pltpu.VMEM((2, 8, 128), jnp.float32),
             pltpu.VMEM((BANDS * 16, 128), jnp.bfloat16),
             pltpu.VMEM((OWNERS * 16, 128), jnp.bfloat16),
             pltpu.VMEM((384, 128), jnp.bfloat16),
@@ -443,7 +508,7 @@
             pltpu.VMEM((18, 8, 8, 128), jnp.float32),
             pltpu.VMEM((6, 8, 8, 128), jnp.float32),
             pltpu.VMEM((BANDS * 16, 128), jnp.bfloat16),
-            pltpu.VMEM((PLANE, 16, 128), jnp.bfloat16),
+            pltpu.VMEM((HOLDERS, 16, 128), jnp.bfloat16),
             pltpu.VMEM((PLANE, 16, 128), jnp.bfloat16),
             pltpu.VMEM((16, 128), jnp.bfloat16),
             pltpu.VMEM((SENDERS, 16, 128), jnp.bfloat16),

time: 73.3 us -> 71.2 us (0.971)
  Pallas kernels: 70.3 us -> 68.2 us
    pallas_call x1, Pallas kernels: 70.3 us -> 68.2 us  [filter_rotate(): pl.pallas_call(functools.partial(filter_rotate_kernel, cells), out_shape=...]
where the time goes in v7:
time: 71.2 us; the launch traced here: 71 us
  Pallas kernels  68.2 us (96%)
  local copies, waits for them, and re-layouts  2.19 us (3%)
    pallas_call x1, Pallas kernels, filter_rotate(): pl.pallas_call(functools.partial(filter_rotate_kernel, cells), out_shape=...  68.2 us
    transpose x1, local copies, waits for them, and re-layouts, body(): tiles.astype(jnp.float32).reshape(size_x, size_y, count, size_z)  1.59 us

profile of v7, /device:TPU:24, one launch (start us, length us, event | category | flops | bytes accessed | tf_op | source)
XLA Modules:
  0.0 71.0 jit_solution(15749375250248418881)
XLA Ops:
  0.6 68.2 %filter_rotate.1 = (bf16[384,128]{1,0:T(8,128)(2,1)}, f32[8,256]{1,0:T(8,128)}) custom-call(f32[8,6,8,128]{3,2,1,0:T(8,128)} %orbitals_ref.1, f32[6,8,128]{2,1,0:T(8,128)} %potential_ref.1), custom_call_target="tpu_custom_call" | custom-call | tf_op jit(solution)/shard_map/filter_rotate/pallas_call | solution.py:487
  68.8 0.0 copy-start
  68.8 1.6 %copy.6 = f32[6,8,8,128]{3,1,0,2:T(8,128)} copy(bf16[6,8,8,128]{3,2,1,0:T(8,128)(2,1)} %bitcast.6) | data formatting | bytes 294912 | tf_op jit(solution)/shard_map/transpose | solution.py:532
  70.4 0.0 copy-done
  70.4 0.6 copy.8
Async XLA Ops:
  68.8 1.6 %copy-start = (f32[8,256]{1,0:T(8,128)S(1)}, f32[8,256]{1,0:T(8,128)}, u32[]{:S(2)}) copy-start(f32[8,256]{1,0:T(8,128)} %get-tuple-element.9) | copy-start | bytes 24580

commit v8 on v7

--- a/solution.py
+++ b/solution.py
@@ -156,17 +156,21 @@
     )
 
 
-def kinetic(wide, other, at):
-    own = wide[6 + at]
-    around = other[at]
-    column = jnp.concatenate([around, own, around], axis=0)
+def along_z(own, shifted):
     total = 3.0 * stencil_coeffs[0] * own
+    for m in range(1, 7):
+        total = total + stencil_coeffs[m] * (pltpu.roll(own, m, 2) + pltpu.roll(own, 128 - m, 2))
+    return shifted * own - 0.5 / spacing**2 * total
+
+
+def across_xy(wide, around, at):
+    column = jnp.concatenate([around, wide[6 + at], around], axis=0)
+    total = jnp.zeros_like(around)
     for m in range(1, 7):
         near = wide[6 + at + m] + wide[6 + at - m]
         near = near + (column[8 + m : 16 + m] + column[8 - m : 16 - m])
-        near = near + (pltpu.roll(own, m, 2) + pltpu.roll(own, 128 - m, 2))
         total = total + stencil_coeffs[m] * near
-    return own, -0.5 / spacing**2 * total
+    return -0.5 / spacing**2 * total
 
 
 def filter_rotate_kernel(
@@ -188,7 +192,7 @@
     halos,
     base,
     slope,
-    other_side,
+    inner,
     shares,
     partial,
     pieces,
@@ -242,7 +246,7 @@
         outgoing[0, rows_at] = plane.reshape(64, 128).astype(jnp.bfloat16)
         return carry
 
-    lax.fori_loop(0, 6, turn, 0)
+    lax.fori_loop(0, 6, turn, 0, unroll=2)
     pl.semaphore_wait(barrier, len(greeted))
     send_tokens(0, (near(0, 0, 3), near(0, 0, -3)))
 
@@ -258,50 +262,61 @@
             device_id_type=MESH,
         )
 
+    def block_rows(at):
+        return pl.ds(pl.multiple_of(at * 64, 64), 64)
+
+    def inner_part(wide):
+        def fill(at, carry):
+            inner[at] = along_z(wide[6 + at], (potential_ref[at] - center)[:, None, :])
+            return carry
+
+        lax.fori_loop(0, 6, fill, 0, unroll=2)
+
     def halo_take(turn_at, wide):
-        for side in range(3):
+        for side in range(2):
             halo_copy(turn_at, side).wait_recv()
 
         def widen(at, carry):
-            rows_at = pl.ds(pl.multiple_of(at * 64, 64), 64)
-            for side, target, offset in ((0, wide, 0), (1, wide, 12), (2, other_side, 0)):
-                block = halos[turn_at, side, rows_at]
-                target[at + offset] = block.astype(jnp.float32).reshape(8, 8, 128)
+            for side in range(2):
+                block = halos[turn_at, side, block_rows(at)]
+                wide[12 * side + at] = block.astype(jnp.float32).reshape(8, 8, 128)
             return carry
 
-        lax.fori_loop(0, 6, widen, 0)
+        lax.fori_loop(0, 6, widen, 0, unroll=2)
+        halo_copy(turn_at, 2).wait_recv()
+
+    def shifted_ham(turn_at, wide, at):
+        around = halos[turn_at, 2, block_rows(at)].astype(jnp.float32).reshape(8, 8, 128)
+        return inner[at] + across_xy(wide, around, at)
 
     half, center, sigma, sigma_two = filter_scalars()
     for side in (2, 0, 1):
         halo_copy(0, side).start()
+    inner_part(base)
     halo_take(0, base)
     pl.semaphore_wait(tokens.at[0], 2)
     send_tokens(1, (near(0, 0, 5), near(0, 0, -5)))
 
     def first_step(at, carry):
-        own, moved = kinetic(base, other_side, at)
-        shifted = (potential_ref[at] - center)[:, None, :]
-        result = sigma / half * (moved + shifted * own)
+        result = sigma / half * shifted_ham(0, base, at)
         slope[6 + at] = result
-        rows_at = pl.ds(pl.multiple_of(at * 64, 64), 64)
-        outgoing[1, rows_at] = result.reshape(64, 128).astype(jnp.bfloat16)
+        outgoing[1, block_rows(at)] = result.reshape(64, 128).astype(jnp.bfloat16)
         return carry
 
-    lax.fori_loop(0, 6, first_step, 0)
+    lax.fori_loop(0, 6, first_step, 0, unroll=2)
     for side in (2, 0, 1):
         halo_copy(1, side).start()
+    inner_part(slope)
     halo_take(1, slope)
     send_tokens(2, (near(3, 0, 0), near(-3, 0, 0)))
 
     def second_step(at, carry):
-        own, moved = kinetic(slope, other_side, at)
-        shifted = (potential_ref[at] - center)[:, None, :]
-        result = 2.0 * sigma_two / half * (moved + shifted * own) - sigma * sigma_two * base[6 + at]
-        rows_at = pl.ds(pl.multiple_of(at * 64, 64), 64)
-        mine_ref[rows_at] = result.reshape(64, 128).astype(jnp.bfloat16)
+        result = 2.0 * sigma_two / half * shifted_ham(1, slope, at)
+        result = result - sigma * sigma_two * base[6 + at]
+        mine_ref[block_rows(at)] = result.reshape(64, 128).astype(jnp.bfloat16)
         return carry
 
-    lax.fori_loop(0, 6, second_step, 0)
+    lax.fori_loop(0, 6, second_step, 0, unroll=2)
 
     def remote(source, target, phase, device):
         return pltpu.make_async_remote_copy(

time: 71.2 us -> 69.5 us (0.976)
  Pallas kernels: 68.2 us -> 66.5 us
    pallas_call x1, Pallas kernels: 68.2 us -> 66.5 us  [filter_rotate(): pl.pallas_call(functools.partial(filter_rotate_kernel, cells), out_shape=...]
where the time goes in v8:
time: 69.5 us; the launch traced here: 69.3 us
  Pallas kernels  66.5 us (96%)
  local copies, waits for them, and re-layouts  2.19 us (3%)
    pallas_call x1, Pallas kernels, filter_rotate(): pl.pallas_call(functools.partial(filter_rotate_kernel, cells), out_shape=...  66.5 us
    transpose x1, local copies, waits for them, and re-layouts, body(): tiles.astype(jnp.float32).reshape(size_x, size_y, count, size_z)  1.59 us

profile of v8, /device:TPU:24, one launch (start us, length us, event | category | flops | bytes accessed | tf_op | source)
XLA Modules:
  0.0 69.3 jit_solution(5716351346366795254)
XLA Ops:
  0.6 66.5 %filter_rotate.1 = (bf16[384,128]{1,0:T(8,128)(2,1)}, f32[8,256]{1,0:T(8,128)}) custom-call(f32[8,6,8,128]{3,2,1,0:T(8,128)} %orbitals_ref.1, f32[6,8,128]{2,1,0:T(8,128)} %potential_ref.1), custom_call_target="tpu_custom_call" | custom-call | tf_op jit(solution)/shard_map/filter_rotate/pallas_call | solution.py:502
  67.1 0.0 copy-start
  67.1 1.6 %copy.6 = f32[6,8,8,128]{3,1,0,2:T(8,128)} copy(bf16[6,8,8,128]{3,2,1,0:T(8,128)(2,1)} %bitcast.6) | data formatting | bytes 294912 | tf_op jit(solution)/shard_map/transpose | solution.py:547
  68.7 0.0 copy-done
  68.7 0.6 copy.8
Async XLA Ops:
  67.1 1.6 %copy-start = (f32[8,256]{1,0:T(8,128)S(1)}, f32[8,256]{1,0:T(8,128)}, u32[]{:S(2)}) copy-start(f32[8,256]{1,0:T(8,128)} %get-tuple-element.9) | copy-start | bytes 24580

commit v9 on v8

--- a/solution.py
+++ b/solution.py
@@ -163,22 +163,30 @@
     return shifted * own - 0.5 / spacing**2 * total
 
 
-def across_xy(wide, around, at):
-    column = jnp.concatenate([around, wide[6 + at], around], axis=0)
-    total = jnp.zeros_like(around)
-    for m in range(1, 7):
-        near = wide[6 + at + m] + wide[6 + at - m]
-        near = near + (column[8 + m : 16 + m] + column[8 - m : 16 - m])
-        total = total + stencil_coeffs[m] * near
+def along_x(wide, at):
+    total = stencil_coeffs[1] * (wide[7 + at] + wide[5 + at])
+    for m in range(2, 7):
+        total = total + stencil_coeffs[m] * (wide[6 + at + m] + wide[6 + at - m])
+    return -0.5 / spacing**2 * total
+
+
+def along_y(own, around):
+    column = jnp.concatenate([around, own, around], axis=0)
+    total = stencil_coeffs[1] * (column[9:17] + column[7:15])
+    for m in range(2, 7):
+        total = total + stencil_coeffs[m] * (column[8 + m : 16 + m] + column[8 - m : 16 - m])
     return -0.5 / spacing**2 * total
 
 
 def filter_rotate_kernel(
     cells,
+    orbitals_hbm,
+    potential_hbm,
+    rotated_hbm,
+    gram_hbm,
     orbitals_ref,
     potential_ref,
-    rotated_ref,
-    gram_ref,
+    gram_rows,
     gram,
     share,
     inverse,
@@ -204,8 +212,13 @@
     halo_recv,
     send_sem,
     recv_sem,
+    local_sem,
     tokens,
 ):
+    load_orbitals = pltpu.make_async_copy(orbitals_hbm, orbitals_ref, local_sem.at[0])
+    load_orbitals.start()
+    load_potential = pltpu.make_async_copy(potential_hbm, potential_ref, local_sem.at[1])
+    load_potential.start()
     band = lax.axis_index("band")
     layer = band % LAYERS
     across = lax.axis_index("gx")
@@ -246,7 +259,9 @@
         outgoing[0, rows_at] = plane.reshape(64, 128).astype(jnp.bfloat16)
         return carry
 
+    load_orbitals.wait()
     lax.fori_loop(0, 6, turn, 0, unroll=2)
+    load_potential.wait()
     pl.semaphore_wait(barrier, len(greeted))
     send_tokens(0, (near(0, 0, 3), near(0, 0, -3)))
 
@@ -283,11 +298,17 @@
             return carry
 
         lax.fori_loop(0, 6, widen, 0, unroll=2)
+
+        def add_x(at, carry):
+            inner[at] = inner[at] + along_x(wide, at)
+            return carry
+
+        lax.fori_loop(0, 6, add_x, 0, unroll=2)
         halo_copy(turn_at, 2).wait_recv()
 
     def shifted_ham(turn_at, wide, at):
         around = halos[turn_at, 2, block_rows(at)].astype(jnp.float32).reshape(8, 8, 128)
-        return inner[at] + across_xy(wide, around, at)
+        return inner[at] + along_y(wide[6 + at], around)
 
     half, center, sigma, sigma_two = filter_scalars()
     for side in (2, 0, 1):
@@ -470,14 +491,9 @@
     gram[:128, 128:] = middle_block.T
     gram[128:, :128] = middle_block
     gram[128:, 128:] = blocks[16:24].reshape(128, 128)
-    gram_ref[...] = gram[pl.ds(pl.multiple_of(band * 8, 8), 8), :]
-
-    await_arrivals(arrived, recv_sem.at[4])
-    rotated_ref[...] = arrived[...]
-
-    @pl.when(owns)
-    def _():
-        await_arrivals(parcels, send_sem.at[4])
+    gram_rows[...] = gram[pl.ds(pl.multiple_of(band * 8, 8), 8), :]
+    store_gram = pltpu.make_async_copy(gram_rows, gram_hbm, local_sem.at[2])
+    store_gram.start()
 
     @pl.when(owns & holds)
     def _():
@@ -496,6 +512,16 @@
     @pl.when(holds)
     def _():
         await_arrivals(blocks.at[pl.ds(0, PLANE - 1)], send_sem.at[3])
+
+    @pl.when(owns)
+    def _():
+        await_arrivals(parcels, send_sem.at[4])
+
+    await_arrivals(arrived, recv_sem.at[4])
+    store_rotated = pltpu.make_async_copy(arrived, rotated_hbm, local_sem.at[3])
+    store_rotated.start()
+    store_gram.wait()
+    store_rotated.wait()
 
 
 def filter_rotate(orbitals, potential, cells):
@@ -505,9 +531,12 @@
             jax.ShapeDtypeStruct((OWNERS * 16, 128), jnp.bfloat16),
             jax.ShapeDtypeStruct((8, FULL), jnp.float32),
         ),
-        in_specs=[pl.BlockSpec(memory_space=pltpu.VMEM)] * 2,
-        out_specs=(pl.BlockSpec(memory_space=pltpu.VMEM),) * 2,
+        in_specs=[pl.BlockSpec(memory_space=pl.ANY)] * 2,
+        out_specs=(pl.BlockSpec(memory_space=pl.ANY),) * 2,
         scratch_shapes=[
+            pltpu.VMEM((8, 6, 8, 128), jnp.float32),
+            pltpu.VMEM((6, 8, 128), jnp.float32),
+            pltpu.VMEM((8, FULL), jnp.float32),
             pltpu.VMEM((FULL, FULL), jnp.float32),
             pltpu.VMEM((FULL, FULL), jnp.bfloat16),
             pltpu.VMEM((128, FULL), jnp.bfloat16),
@@ -533,6 +562,7 @@
             pltpu.SemaphoreType.DMA((2, 3)),
             pltpu.SemaphoreType.DMA((5,)),
             pltpu.SemaphoreType.DMA((5,)),
+            pltpu.SemaphoreType.DMA((4,)),
             pltpu.SemaphoreType.REGULAR((3,)),
         ],
         compiler_params=pltpu.CompilerParams(collective_id=1, has_side_effects=True),

time: 69.5 us -> 68.5 us (0.986)
  Pallas kernels: 66.5 us -> 65.5 us
    pallas_call x1, Pallas kernels: 66.5 us -> 65.5 us  [filter_rotate(): pl.pallas_call(functools.partial(filter_rotate_kernel, cells), out_shape=...]
where the time goes in v9:
time: 68.5 us; the launch traced here: 68.3 us
  Pallas kernels  65.5 us (96%)
  local copies, waits for them, and re-layouts  2.19 us (3%)
    pallas_call x1, Pallas kernels, filter_rotate(): pl.pallas_call(functools.partial(filter_rotate_kernel, cells), out_shape=...  65.5 us
    transpose x1, local copies, waits for them, and re-layouts, body(): tiles.astype(jnp.float32).reshape(size_x, size_y, count, size_z)  1.59 us

profile of v9, /device:TPU:24, one launch (start us, length us, event | category | flops | bytes accessed | tf_op | source)
XLA Modules:
  0.0 68.3 jit_solution(4558999079452507076)
XLA Ops:
  0.6 65.5 %filter_rotate.1 = (bf16[384,128]{1,0:T(8,128)(2,1)}, f32[8,256]{1,0:T(8,128)}) custom-call(f32[8,6,8,128]{3,2,1,0:T(8,128)} %orbitals_hbm.1, f32[6,8,128]{2,1,0:T(8,128)} %potential_hbm.1), custom_call_target="tpu_custom_call" | custom-call | tf_op jit(solution)/shard_map/filter_rotate/pallas_call | solution.py:528
  66.1 0.0 copy-start
  66.2 1.6 %copy.6 = f32[6,8,8,128]{3,1,0,2:T(8,128)} copy(bf16[6,8,8,128]{3,2,1,0:T(8,128)(2,1)} %bitcast.6) | data formatting | bytes 294912 | tf_op jit(solution)/shard_map/transpose | solution.py:577
  67.7 0.0 copy-done
  67.7 0.6 copy.8
Async XLA Ops:
  66.1 1.6 %copy-start = (f32[8,256]{1,0:T(8,128)S(1)}, f32[8,256]{1,0:T(8,128)}, u32[]{:S(2)}) copy-start(f32[8,256]{1,0:T(8,128)} %get-tuple-element.9) | copy-start | bytes 24580

commit v10 on v9

--- a/solution.py
+++ b/solution.py
@@ -570,12 +570,31 @@
     )(orbitals, potential)
 
 
+def place_kernel(tiles_ref, rows_ref, rotated_ref, gram_ref):
+    gram_ref[...] = rows_ref[...]
+    for at in range(6):
+        plane = tiles_ref[64 * at : 64 * at + 64].astype(jnp.float32).reshape(8, 8, 128)
+        rotated_ref[:, at] = jnp.swapaxes(plane, 0, 1)
+
+
+def place_outputs(tiles, rows, shape):
+    return pl.pallas_call(
+        place_kernel,
+        out_shape=(
+            jax.ShapeDtypeStruct(shape, jnp.float32),
+            jax.ShapeDtypeStruct(rows.shape, jnp.float32),
+        ),
+        in_specs=[pl.BlockSpec(memory_space=pltpu.VMEM)] * 2,
+        out_specs=(pl.BlockSpec(memory_space=pltpu.VMEM),) * 2,
+        name="place_outputs",
+    )(tiles, rows)
+
+
 def body(orbitals, potential):
     count, size_x, size_y, size_z = orbitals.shape
     total_cells = size_x * size_y * size_z * lax.axis_size("gx") * lax.axis_size("gy")
     tiles, gram_rows = filter_rotate(orbitals, potential, float(total_cells))
-    rotated = tiles.astype(jnp.float32).reshape(size_x, size_y, count, size_z).transpose(2, 0, 1, 3)
-    return (rotated, gram_rows)
+    return place_outputs(tiles, gram_rows, orbitals.shape)
 
 
 def solution(mesh):

time: 68.5 us -> 67.9 us (level)
  local copies, waits for them, and re-layouts: 2.19 us -> 0 us
  Pallas kernels: 65.5 us -> 67.1 us
    pallas_call x0 -> x1, Pallas kernels: none -> 1.62 us  [place_outputs(): pl.pallas_call(place_kernel, out_shape=(jax.ShapeDtypeStruct(shape, jnp.f...]
    transpose x1 -> x0, local copies, waits for them, and re-layouts: 1.59 us -> none  [body(): tiles.astype(jnp.float32).reshape(size_x, size_y, count, size_z)]
where the time goes in v10:
time: 67.9 us; the launch traced here: 67.8 us
  Pallas kernels  67.1 us (99%)
    pallas_call x1, Pallas kernels, filter_rotate(): pl.pallas_call(functools.partial(filter_rotate_kernel, cells), out_shape=...  65.5 us
    pallas_call x1, Pallas kernels, place_outputs(): pl.pallas_call(place_kernel, out_shape=(jax.ShapeDtypeStruct(shape, jnp.f...  1.62 us

profile of v10, /device:TPU:24, one launch (start us, length us, event | category | flops | bytes accessed | tf_op | source)
XLA Modules:
  0.0 67.8 jit_solution(3326000443001808155)
XLA Ops:
  0.6 65.5 %filter_rotate.1 = (bf16[384,128]{1,0:T(8,128)(2,1)}, f32[8,256]{1,0:T(8,128)}) custom-call(f32[8,6,8,128]{3,2,1,0:T(8,128)} %orbitals_hbm.1, f32[6,8,128]{2,1,0:T(8,128)} %potential_hbm.1), custom_call_target="tpu_custom_call" | custom-call | tf_op jit(solution)/shard_map/filter_rotate/pallas_call | solution.py:528
  66.2 1.6 %place_outputs.1 = (f32[8,6,8,128]{3,2,1,0:T(8,128)}, f32[8,256]{1,0:T(8,128)}) custom-call(bf16[384,128]{1,0:T(8,128)(2,1)} %get-tuple-element.4.tiles_ref, f32[8,256]{1,0:T(8,128)} %get-tuple-element.5.rows_ref), custom_call_target="tpu_custom_call" | custom-call | tf_op jit(solution)/shard_map/place_outputs/pallas_call | solution.py:581

commit v11 on v10

--- a/solution.py
+++ b/solution.py
@@ -182,11 +182,10 @@
     cells,
     orbitals_hbm,
     potential_hbm,
-    rotated_hbm,
-    gram_hbm,
+    rotated_ref,
+    gram_ref,
     orbitals_ref,
     potential_ref,
-    gram_rows,
     gram,
     share,
     inverse,
@@ -491,9 +490,7 @@
     gram[:128, 128:] = middle_block.T
     gram[128:, :128] = middle_block
     gram[128:, 128:] = blocks[16:24].reshape(128, 128)
-    gram_rows[...] = gram[pl.ds(pl.multiple_of(band * 8, 8), 8), :]
-    store_gram = pltpu.make_async_copy(gram_rows, gram_hbm, local_sem.at[2])
-    store_gram.start()
+    gram_ref[...] = gram[pl.ds(pl.multiple_of(band * 8, 8), 8), :]
 
     @pl.when(owns & holds)
     def _():
@@ -518,25 +515,21 @@
         await_arrivals(parcels, send_sem.at[4])
 
     await_arrivals(arrived, recv_sem.at[4])
-    store_rotated = pltpu.make_async_copy(arrived, rotated_hbm, local_sem.at[3])
-    store_rotated.start()
-    store_gram.wait()
-    store_rotated.wait()
+    rotated_ref[...] = arrived[...]
 
 
 def filter_rotate(orbitals, potential, cells):
     return pl.pallas_call(
         functools.partial(filter_rotate_kernel, cells),
         out_shape=(
-            jax.ShapeDtypeStruct((OWNERS * 16, 128), jnp.bfloat16),
-            jax.ShapeDtypeStruct((8, FULL), jnp.float32),
+            pltpu.VMEM((OWNERS * 16, 128), jnp.bfloat16),
+            pltpu.VMEM((8, FULL), jnp.float32),
         ),
         in_specs=[pl.BlockSpec(memory_space=pl.ANY)] * 2,
-        out_specs=(pl.BlockSpec(memory_space=pl.ANY),) * 2,
+        out_specs=(pl.BlockSpec(memory_space=pltpu.VMEM),) * 2,
         scratch_shapes=[
             pltpu.VMEM((8, 6, 8, 128), jnp.float32),
             pltpu.VMEM((6, 8, 128), jnp.float32),
-            pltpu.VMEM((8, FULL), jnp.float32),
             pltpu.VMEM((FULL, FULL), jnp.float32),
             pltpu.VMEM((FULL, FULL), jnp.bfloat16),
             pltpu.VMEM((128, FULL), jnp.bfloat16),
@@ -562,7 +555,7 @@
             pltpu.SemaphoreType.DMA((2, 3)),
             pltpu.SemaphoreType.DMA((5,)),
             pltpu.SemaphoreType.DMA((5,)),
-            pltpu.SemaphoreType.DMA((4,)),
+            pltpu.SemaphoreType.DMA((2,)),
             pltpu.SemaphoreType.REGULAR((3,)),
         ],
         compiler_params=pltpu.CompilerParams(collective_id=1, has_side_effects=True),
@@ -587,7 +580,7 @@
         in_specs=[pl.BlockSpec(memory_space=pltpu.VMEM)] * 2,
         out_specs=(pl.BlockSpec(memory_space=pltpu.VMEM),) * 2,
         name="place_outputs",
-    )(tiles, rows)
+    )(*(pltpu.with_memory_space_constraint(part, pltpu.VMEM) for part in (tiles, rows)))
 
 
 def body(orbitals, potential):

time: 67.9 us -> 66.4 us (0.978)
  Pallas kernels: 67.1 us -> 65.6 us
    pallas_call x1, Pallas kernels: 1.62 us -> 0.72 us  [place_outputs(): pl.pallas_call(place_kernel, out_shape=(jax.ShapeDtypeStruct(shape, jnp.f...]
where the time goes in v11:
time: 66.4 us; the launch traced here: 66.2 us
  Pallas kernels  65.6 us (99%)
    pallas_call x1, Pallas kernels, filter_rotate(): pl.pallas_call(functools.partial(filter_rotate_kernel, cells), out_shape=...  64.9 us

profile of v11, /device:TPU:24, one launch (start us, length us, event | category | flops | bytes accessed | tf_op | source)
XLA Modules:
  0.0 66.2 jit_solution(2849603994259225894)
XLA Ops:
  0.6 64.9 %filter_rotate.1 = (bf16[384,128]{1,0:T(8,128)(2,1)S(1)}, f32[8,256]{1,0:T(8,128)S(1)}) custom-call(f32[8,6,8,128]{3,2,1,0:T(8,128)} %orbitals_hbm.1, f32[6,8,128]{2,1,0:T(8,128)} %potential_hbm.1), custom_call_target="tpu_custom_call" | custom-call | tf_op jit(solution)/shard_map/filter_rotate/pallas_call | solution.py:522
  65.5 0.7 %place_outputs.1 = (f32[8,6,8,128]{3,2,1,0:T(8,128)}, f32[8,256]{1,0:T(8,128)}) custom-call(bf16[384,128]{1,0:T(8,128)(2,1)S(1)} %get-tuple-element.4.tiles_ref, f32[8,256]{1,0:T(8,128)S(1)} %get-tuple-element.5.rows_ref), custom_call_target="tpu_custom_call" | custom-call | tf_op jit(solution)/shard_map/place_outputs/pallas_call | solution.py:574

commit v12 on v11

--- a/solution.py
+++ b/solution.py
@@ -234,6 +234,7 @@
 
     holds = holds_piece(across, row)
     own_piece = piece_of(across, row)
+    leads = own_piece < 8
 
     def near(step_x, step_y, step_z):
         return spot(
@@ -431,20 +432,42 @@
     def _():
         total[...] = jnp.sum(layers[...].astype(jnp.float32), axis=0) / cells
 
-        def send_total(step, carry):
-            other = plane_partner(place, step)
-            remote(
-                total, blocks.at[own_piece], 3, spot(other // GRID_Y, other % GRID_Y, layer)
-            ).start()
-            return carry
-
-        lax.fori_loop(0, PLANE - 1, send_total, 0)
+        def send_totals(phase):
+            def send_total(step, carry):
+                other = plane_partner(place, step)
+                remote(
+                    total,
+                    blocks.at[own_piece],
+                    phase,
+                    spot(other // GRID_Y, other % GRID_Y, layer),
+                ).start()
+                return carry
+
+            lax.fori_loop(0, PLANE - 1, send_total, 0)
+
+        @pl.when(leads)
+        def _():
+            send_totals(3)
+
+        @pl.when(jnp.logical_not(leads))
+        def _():
+            send_totals(5)
+
         blocks[own_piece] = total[...]
-        await_arrivals(blocks.at[pl.ds(0, HOLDERS - 1)], recv_sem.at[3])
-
-    @pl.when(jnp.logical_not(holds))
-    def _():
-        await_arrivals(blocks.at[pl.ds(0, HOLDERS)], recv_sem.at[3])
+
+    def await_blocks(own, begin, count, phase):
+        @pl.when(own)
+        def _():
+            await_arrivals(blocks.at[pl.ds(begin, count - 1)], recv_sem.at[phase])
+
+        @pl.when(jnp.logical_not(own))
+        def _():
+            await_arrivals(blocks.at[pl.ds(begin, count)], recv_sem.at[phase])
+
+    await_blocks(holds & leads, 0, 8, 3)
+
+    def await_rest():
+        await_blocks(holds & jnp.logical_not(leads), 8, 16, 5)
 
     @pl.when(owns)
     def _():
@@ -474,10 +497,10 @@
             lax.fori_loop(0, LAYERS, send_parcel, 0)
 
         buffers = (rows_buf, cols_buf, panel_buf)
-        corner = blocks[8:16].reshape(128, 128)
         upper = inverse_factor(blocks[0:8].reshape(128, 128), *buffers)
         send_parcels(0, upper.astype(jnp.bfloat16), share[:128])
-        lower_left = full_dot(corner, upper, 1, 1)
+        await_rest()
+        lower_left = full_dot(blocks[8:16].reshape(128, 128), upper, 1, 1)
         remaining = blocks[16:24].reshape(128, 128) - full_dot(lower_left, lower_left, 1, 1)
         carried = full_dot(lower_left, upper, 1, 0)
         lower = inverse_factor(remaining, *buffers)
@@ -485,6 +508,10 @@
         inverse[:, :128] = (-full_dot(lower, carried, 1, 0)).astype(jnp.bfloat16)
         send_parcels(1, inverse[...], share[...])
 
+    @pl.when(jnp.logical_not(owns))
+    def _():
+        await_rest()
+
     middle_block = blocks[8:16].reshape(128, 128)
     gram[:128, :128] = blocks[0:8].reshape(128, 128)
     gram[:128, 128:] = middle_block.T
@@ -506,9 +533,13 @@
         for side in range(3):
             halo_copy(turn_at, side).wait_send()
 
-    @pl.when(holds)
+    @pl.when(holds & leads)
     def _():
         await_arrivals(blocks.at[pl.ds(0, PLANE - 1)], send_sem.at[3])
+
+    @pl.when(holds & jnp.logical_not(leads))
+    def _():
+        await_arrivals(blocks.at[pl.ds(0, PLANE - 1)], send_sem.at[5])
 
     @pl.when(owns)
     def _():
@@ -553,8 +584,8 @@
             pltpu.VMEM((PLANE, 16, 128), jnp.float32),
             pltpu.SemaphoreType.DMA((2, 3)),
             pltpu.SemaphoreType.DMA((2, 3)),
-            pltpu.SemaphoreType.DMA((5,)),
-            pltpu.SemaphoreType.DMA((5,)),
+            pltpu.SemaphoreType.DMA((6,)),
+            pltpu.SemaphoreType.DMA((6,)),
             pltpu.SemaphoreType.DMA((2,)),
             pltpu.SemaphoreType.REGULAR((3,)),
         ],

time: 66.4 us -> 66.1 us (level)
  no operation moved by 1% of the time
where the time goes in v12:
time: 66.1 us; the launch traced here: 65.9 us
  Pallas kernels  65.3 us (99%)
    pallas_call x1, Pallas kernels, filter_rotate(): pl.pallas_call(functools.partial(filter_rotate_kernel, cells), out_shape=...  64.6 us

profile of v12, /device:TPU:24, one launch (start us, length us, event | category | flops | bytes accessed | tf_op | source)
XLA Modules:
  0.0 65.9 jit_solution(4020281993374311442)
XLA Ops:
  0.6 64.6 %filter_rotate.1 = (bf16[384,128]{1,0:T(8,128)(2,1)S(1)}, f32[8,256]{1,0:T(8,128)S(1)}) custom-call(f32[8,6,8,128]{3,2,1,0:T(8,128)} %orbitals_hbm.1, f32[6,8,128]{2,1,0:T(8,128)} %potential_hbm.1), custom_call_target="tpu_custom_call" | custom-call | tf_op jit(solution)/shard_map/filter_rotate/pallas_call | solution.py:553
  65.2 0.7 %place_outputs.1 = (f32[8,6,8,128]{3,2,1,0:T(8,128)}, f32[8,256]{1,0:T(8,128)}) custom-call(bf16[384,128]{1,0:T(8,128)(2,1)S(1)} %get-tuple-element.4.tiles_ref, f32[8,256]{1,0:T(8,128)S(1)} %get-tuple-element.5.rows_ref), custom_call_target="tpu_custom_call" | custom-call | tf_op jit(solution)/shard_map/place_outputs/pallas_call | solution.py:605

commit v13 on v11

--- a/solution.py
+++ b/solution.py
@@ -75,7 +75,7 @@
     return high, middle, (rest - middle.astype(jnp.float32)).astype(jnp.bfloat16)
 
 
-def inverse_factor(matrix, rows_buf, cols_buf, panel_buf):
+def inverse_factor(matrix, rows_buf, cols_buf, panel_buf, at_half=None):
     tile, size = 8, 128
     count = size // tile
     lane = lax.broadcasted_iota(jnp.int32, (tile, size), 1)
@@ -142,6 +142,8 @@
                 for p in range(tile):
                     value = value - full(tiles[t][:, begin + p : begin + p + 1]) * solved[p]
                 tiles[t] = value
+        if at_half is not None and 2 * (now + 1) == count:
+            at_half(jnp.concatenate(done, axis=0))
     return jnp.concatenate(done, axis=0)
 
 
@@ -188,7 +190,6 @@
     potential_ref,
     gram,
     share,
-    inverse,
     rows_buf,
     cols_buf,
     panel_buf,
@@ -450,40 +451,49 @@
     def _():
         to = pl.multiple_of(band_share(band) * 16, 16)
 
-        def send_parcels(side, weights, cells_of):
+        def send_parcels(first, count, weights, cells_of):
             turned = jnp.dot(weights, cells_of, preferred_element_type=jnp.float32)
             halves = [
-                turned[:, 128 * h : 128 * h + 128].reshape(LAYERS, 1, 8, 128) for h in range(2)
+                turned[:, 128 * h : 128 * h + 128].reshape(count, 1, 8, 128) for h in range(2)
             ]
-            base_row = side * LAYERS * 16
-            parcels[base_row : base_row + LAYERS * 16] = (
-                jnp.concatenate(halves, axis=1).reshape(LAYERS * 16, 128).astype(jnp.bfloat16)
+            parcels[first * 16 : (first + count) * 16] = (
+                jnp.concatenate(halves, axis=1).reshape(count * 16, 128).astype(jnp.bfloat16)
             )
 
             def send_parcel(step, carry):
-                other = side * LAYERS + (layer + far_first(step, LAYERS)) % LAYERS
-                at = pl.multiple_of(other * 16, 16)
-                remote(
-                    parcels.at[pl.ds(at, 16)],
-                    arrived.at[pl.ds(to, 16)],
-                    4,
-                    {"band": other, "gy": 1 - half_y},
-                ).start()
+                offset = (layer + far_first(step, LAYERS)) % LAYERS
+                low = first % LAYERS
+
+                @pl.when((offset >= low) & (offset < low + count))
+                def _():
+                    other = (first // LAYERS) * LAYERS + offset
+                    at = pl.multiple_of(other * 16, 16)
+                    remote(
+                        parcels.at[pl.ds(at, 16)],
+                        arrived.at[pl.ds(to, 16)],
+                        4,
+                        {"band": other, "gy": 1 - half_y},
+                    ).start()
+
                 return carry
 
             lax.fori_loop(0, LAYERS, send_parcel, 0)
 
         buffers = (rows_buf, cols_buf, panel_buf)
+        upper = inverse_factor(blocks[0:8].reshape(128, 128), *buffers)
+        send_parcels(0, 16, upper.astype(jnp.bfloat16), share[:128])
         corner = blocks[8:16].reshape(128, 128)
-        upper = inverse_factor(blocks[0:8].reshape(128, 128), *buffers)
-        send_parcels(0, upper.astype(jnp.bfloat16), share[:128])
         lower_left = full_dot(corner, upper, 1, 1)
         remaining = blocks[16:24].reshape(128, 128) - full_dot(lower_left, lower_left, 1, 1)
         carried = full_dot(lower_left, upper, 1, 0)
-        lower = inverse_factor(remaining, *buffers)
-        inverse[:, 128:] = lower.astype(jnp.bfloat16)
-        inverse[:, :128] = (-full_dot(lower, carried, 1, 0)).astype(jnp.bfloat16)
-        send_parcels(1, inverse[...], share[...])
+
+        def send_lower(first, rows):
+            left = -full_dot(rows, carried, 1, 0)
+            weights = jnp.concatenate([left, rows], axis=1).astype(jnp.bfloat16)
+            send_parcels(first, 8, weights, share[...])
+
+        lower = inverse_factor(remaining, *buffers, lambda rows: send_lower(16, rows))
+        send_lower(24, lower[64:])
 
     middle_block = blocks[8:16].reshape(128, 128)
     gram[:128, :128] = blocks[0:8].reshape(128, 128)
@@ -532,7 +542,6 @@
             pltpu.VMEM((6, 8, 128), jnp.float32),
             pltpu.VMEM((FULL, FULL), jnp.float32),
             pltpu.VMEM((FULL, FULL), jnp.bfloat16),
-            pltpu.VMEM((128, FULL), jnp.bfloat16),
             pltpu.VMEM((2, 8, 128), jnp.float32),
             pltpu.VMEM((2, 8, 8, 128), jnp.float32),
             pltpu.VMEM((2, 8, 128), jnp.float32),

time: 66.4 us -> 64.8 us (0.976)
  Pallas kernels: 65.6 us -> 64 us
    pallas_call x1, Pallas kernels: 64.9 us -> 63.3 us  [filter_rotate(): pl.pallas_call(functools.partial(filter_rotate_kernel, cells), out_shape=...]
where the time goes in v13:
time: 64.8 us; the launch traced here: 64.7 us
  Pallas kernels  64 us (99%)
    pallas_call x1, Pallas kernels, filter_rotate(): pl.pallas_call(functools.partial(filter_rotate_kernel, cells), out_shape=...  63.3 us

profile of v13, /device:TPU:24, one launch (start us, length us, event | category | flops | bytes accessed | tf_op | source)
XLA Modules:
  0.0 64.7 jit_solution(15327235911981833205)
XLA Ops:
  0.6 63.3 %filter_rotate.1 = (bf16[384,128]{1,0:T(8,128)(2,1)S(1)}, f32[8,256]{1,0:T(8,128)S(1)}) custom-call(f32[8,6,8,128]{3,2,1,0:T(8,128)} %orbitals_hbm.1, f32[6,8,128]{2,1,0:T(8,128)} %potential_hbm.1), custom_call_target="tpu_custom_call" | custom-call | tf_op jit(solution)/shard_map/filter_rotate/pallas_call | solution.py:532
  63.9 0.7 %place_outputs.1 = (f32[8,6,8,128]{3,2,1,0:T(8,128)}, f32[8,256]{1,0:T(8,128)}) custom-call(bf16[384,128]{1,0:T(8,128)(2,1)S(1)} %get-tuple-element.4.tiles_ref, f32[8,256]{1,0:T(8,128)S(1)} %get-tuple-element.5.rows_ref), custom_call_target="tpu_custom_call" | custom-call | tf_op jit(solution)/shard_map/place_outputs/pallas_call | solution.py:583

commit v14 on v13

--- a/solution.py
+++ b/solution.py
@@ -75,7 +75,7 @@
     return high, middle, (rest - middle.astype(jnp.float32)).astype(jnp.bfloat16)
 
 
-def inverse_factor(matrix, rows_buf, cols_buf, panel_buf, at_half=None):
+def inverse_factor(matrix, rows_buf, cols_buf, panel_buf, part_ready=None):
     tile, size = 8, 128
     count = size // tile
     lane = lax.broadcasted_iota(jnp.int32, (tile, size), 1)
@@ -142,8 +142,8 @@
                 for p in range(tile):
                     value = value - full(tiles[t][:, begin + p : begin + p + 1]) * solved[p]
                 tiles[t] = value
-        if at_half is not None and 2 * (now + 1) == count:
-            at_half(jnp.concatenate(done, axis=0))
+        if part_ready is not None:
+            part_ready(done)
     return jnp.concatenate(done, axis=0)
 
 
@@ -487,13 +487,15 @@
         remaining = blocks[16:24].reshape(128, 128) - full_dot(lower_left, lower_left, 1, 1)
         carried = full_dot(lower_left, upper, 1, 0)
 
-        def send_lower(first, rows):
-            left = -full_dot(rows, carried, 1, 0)
-            weights = jnp.concatenate([left, rows], axis=1).astype(jnp.bfloat16)
-            send_parcels(first, 8, weights, share[...])
-
-        lower = inverse_factor(remaining, *buffers, lambda rows: send_lower(16, rows))
-        send_lower(24, lower[64:])
+        def send_lower(done):
+            for begin, end in ((0, 8), (8, 12), (12, 16)):
+                if len(done) == end:
+                    rows = jnp.concatenate(done[begin:], axis=0)
+                    left = -full_dot(rows, carried, 1, 0)
+                    weights = jnp.concatenate([left, rows], axis=1).astype(jnp.bfloat16)
+                    send_parcels(LAYERS + begin, end - begin, weights, share[...])
+
+        inverse_factor(remaining, *buffers, send_lower)
 
     middle_block = blocks[8:16].reshape(128, 128)
     gram[:128, :128] = blocks[0:8].reshape(128, 128)

time: 64.8 us -> 64.8 us (level)
  no operation moved by 1% of the time
where the time goes in v14:
time: 64.8 us; the launch traced here: 64.7 us
  Pallas kernels  64 us (99%)
    pallas_call x1, Pallas kernels, filter_rotate(): pl.pallas_call(functools.partial(filter_rotate_kernel, cells), out_shape=...  63.3 us

profile of v14, /device:TPU:24, one launch (start us, length us, event | category | flops | bytes accessed | tf_op | source)
XLA Modules:
  0.0 64.7 jit_solution(10637709871933615041)
XLA Ops:
  0.6 63.3 %filter_rotate.1 = (bf16[384,128]{1,0:T(8,128)(2,1)S(1)}, f32[8,256]{1,0:T(8,128)S(1)}) custom-call(f32[8,6,8,128]{3,2,1,0:T(8,128)} %orbitals_hbm.1, f32[6,8,128]{2,1,0:T(8,128)} %potential_hbm.1), custom_call_target="tpu_custom_call" | custom-call | tf_op jit(solution)/shard_map/filter_rotate/pallas_call | solution.py:534
  63.9 0.7 %place_outputs.1 = (f32[8,6,8,128]{3,2,1,0:T(8,128)}, f32[8,256]{1,0:T(8,128)}) custom-call(bf16[384,128]{1,0:T(8,128)(2,1)S(1)} %get-tuple-element.4.tiles_ref, f32[8,256]{1,0:T(8,128)S(1)} %get-tuple-element.5.rows_ref), custom_call_target="tpu_custom_call" | custom-call | tf_op jit(solution)/shard_map/place_outputs/pallas_call | solution.py:585
